TPU v7x, 32 devices: a whole 2x2x4 slice. The times are simulated.
32 devices in a mesh: parts: 2 (over x), lat: 16 (over z, y, core).
Axes of the slice: x: 2, y: 2, z: 4, core: 2. Of those that a mesh axis runs over, the one named last changes fastest.
Arguments:
- grid_field: float32 [368, 1440, 256], P('lat', None, 'parts'), parts along dimension 2, may hold values from -170 to 170
- norm_gain: float32 [128], P('parts'), parts along dimension 0, may hold values from 0.5 to 1.5
- filter_weight: bfloat16 [352, 2, 64, 128], P('lat', None, None, 'parts'), parts along dimension 3, may hold values from -0.5 to 0.5
Outputs:
- spectrum_out: bfloat16 [352, 352, 512], P('lat', None, 'parts'), parts along dimension 2
There are 2 independent parts, one for each index of `parts`. A program takes and returns all parts, laid end to end along the dimension named above; each array names one. Nothing has to cross between parts.
All inputs are finite; a program needn't handle non-finite values.
Results may differ from a plain program's by a relative error of at most 0.0064.
Values may be sent and summed in bfloat16 or wider, within the bound.
A program may use at most 192 MiB of HBM per device.

v0:
```python
import math

import jax
import jax.numpy as jnp
import numpy as np
from jax import lax
from jax.experimental import pallas as pl
from jax.experimental.pallas import tpu as pltpu
from jax.sharding import PartitionSpec as P

C = 64
S = 2
DEG_DEV = 22
ORDER_PAD = 24
BLOCK = 16
LANES = 128


def round_up(value, step):
    return -(-value // step) * step


def legendre_kernel(
    orders_ref, cosine_ref, weights_ref, mant_ref, exp_ref, out_ref, prev_ref, early_ref, grow_ref, rows_ref
):
    block = pl.program_id(0)
    width = cosine_ref.shape[1]
    kept_width = out_ref.shape[2]

    @pl.when(block == 0)
    def _():
        prev_ref[...] = jnp.zeros_like(prev_ref)
        early_ref[...] = jnp.zeros_like(early_ref)
        grow_ref[...] = jnp.zeros_like(grow_ref)

    orders = orders_ref[...]
    narrow = orders[:, :LANES]
    order_sq = narrow * narrow
    cosine = cosine_ref[...]
    weights = weights_ref[...]
    limit = 2.0**64
    shrink = 2.0 ** (-64)
    previous, earlier, exponent = prev_ref[...], early_ref[...], grow_ref[...]
    first = (block * BLOCK).astype(jnp.float32)

    def widen(value):
        return jnp.concatenate([value] * (width // LANES), axis=1)

    for step in range(BLOCK):
        degree = first + float(step)
        upper = jnp.sqrt(
            (4.0 * degree * degree - 1.0) / jnp.maximum(degree * degree - order_sq, 1.0)
        )
        below = degree - 1.0
        lower = jnp.sqrt(
            jnp.maximum(below * below - order_sq, 0.0)
            / jnp.maximum(jnp.full_like(order_sq, 4.0 * below * below - 1.0), 1.0)
        )
        recurred = widen(upper) * (cosine * previous - widen(lower) * earlier)
        at_start = orders == degree
        current = jnp.where(at_start, mant_ref[...], jnp.where(orders < degree, recurred, 0.0))
        exponent = jnp.where(at_start, exp_ref[...], exponent)
        value = weights * (current * jnp.exp2(exponent))
        for lane in range(width // LANES):
            rows_ref[lane, step * ORDER_PAD : (step + 1) * ORDER_PAD, :] = value[
                :, lane * LANES : (lane + 1) * LANES
            ]
        large = jnp.abs(current) > limit
        earlier = jnp.where(large, previous * shrink, previous)
        previous = jnp.where(large, current * shrink, current)
        exponent = jnp.where(large, exponent + 64.0, exponent)

    prev_ref[...] = previous
    early_ref[...] = earlier
    grow_ref[...] = exponent
    for order in range(DEG_DEV):
        for lane in range(0, width, LANES):
            cut = min(LANES, kept_width - lane)
            piece = rows_ref[lane // LANES, pl.ds(order, BLOCK, stride=ORDER_PAD), :]
            out_ref[order, :, lane : lane + cut] = piece[:, :cut].astype(out_ref.dtype)


def legendre_table(colatitude, first_order, degrees, weight_scale):
    rows = colatitude.shape[0]
    width = round_up(rows, LANES)
    colat = jnp.concatenate([colatitude, jnp.full((width - rows,), 0.5 * math.pi, jnp.float32)])
    orders = (first_order + jnp.arange(ORDER_PAD, dtype=jnp.int32)).astype(jnp.float32)
    sine_rows = jnp.sin(colat)
    log_start = 0.5 * jnp.log((2.0 * orders + 1.0) / (4.0 * math.pi)) + 0.5 * (
        lax.lgamma(orders + 0.5) - lax.lgamma(orders + 1.0) - 0.5 * math.log(math.pi)
    )
    log_diag = log_start[:, None] + orders[:, None] * jnp.log(sine_rows)[None, :]
    start_exp = 64.0 * jnp.floor(log_diag / (64.0 * math.log(2.0)))
    start_mant = jnp.exp(log_diag - start_exp * math.log(2.0))
    state = (ORDER_PAD, width)
    whole = pl.BlockSpec(state, lambda i: (0, 0))
    line = pl.BlockSpec((1, width), lambda i: (0, 0))
    return pl.pallas_call(
        legendre_kernel,
        grid=(degrees // BLOCK,),
        out_shape=jax.ShapeDtypeStruct((DEG_DEV, degrees, rows), jnp.bfloat16),
        in_specs=[whole, line, line, whole, whole],
        out_specs=pl.BlockSpec((DEG_DEV, BLOCK, rows), lambda i: (0, i, 0)),
        scratch_shapes=[
            pltpu.VMEM(state, jnp.float32),
            pltpu.VMEM(state, jnp.float32),
            pltpu.VMEM(state, jnp.float32),
            pltpu.VMEM((width // LANES, BLOCK * ORDER_PAD, LANES), jnp.float32),
        ],
        cost_estimate=pl.CostEstimate(
            flops=degrees * ORDER_PAD * width * 2000,
            bytes_accessed=DEG_DEV * degrees * rows * 2,
            transcendentals=degrees * ORDER_PAD * width,
        ),
        compiler_params=pltpu.CompilerParams(vmem_limit_bytes=24 * 1024 * 1024),
    )(
        jnp.broadcast_to(orders[:, None], state),
        jnp.cos(colat)[None, :],
        (weight_scale * sine_rows)[None, :],
        start_mant,
        start_exp,
    )


def expand_filter(filter_weight):
    real_part = filter_weight[:, 0]
    imag_part = filter_weight[:, 1]
    from_real = jnp.stack([real_part, imag_part], axis=1)
    from_imag = jnp.stack([-imag_part, real_part], axis=1)
    mixing = jnp.stack([from_real, from_imag], axis=1)
    same = jnp.eye(S, dtype=filter_weight.dtype)
    full = mixing.transpose(0, 1, 3, 2, 4)[:, :, None, :, :, None, :] * same[None, None, :, None, None, :, None]
    return full.reshape(filter_weight.shape[0], 2 * S * C, 2 * S * C)


def mix_kernel(sin_ref, cos_ref, weight_ref, out_ref, rows_ref):
    sources, degrees, orders, half = cos_ref.shape
    for degree in range(degrees):
        for source in range(sources):
            rows = slice(source * orders, (source + 1) * orders)
            rows_ref[degree, rows, :half] = cos_ref[source, degree].astype(jnp.float32)
            rows_ref[degree, rows, half:] = sin_ref[source, degree].astype(jnp.float32)
        out_ref[degree] = jnp.dot(
            rows_ref[degree].astype(jnp.bfloat16),
            weight_ref[degree],
            preferred_element_type=jnp.float32,
        ).astype(out_ref.dtype)


def mix(coef_sin, coef_cos, weights):
    sources, degrees, orders, half = coef_cos.shape
    wide = weights.shape[2]
    step = 2
    piece = pl.BlockSpec((sources, step, orders, half), lambda i: (0, i, 0, 0))
    return pl.pallas_call(
        mix_kernel,
        grid=(degrees // step,),
        out_shape=jax.ShapeDtypeStruct((degrees, sources * orders, wide), jnp.bfloat16),
        in_specs=[piece, piece, pl.BlockSpec((step, 2 * half, wide), lambda i: (i, 0, 0))],
        out_specs=pl.BlockSpec((step, sources * orders, wide), lambda i: (i, 0, 0)),
        scratch_shapes=[pltpu.VMEM((step, sources * orders, 2 * half), jnp.float32)],
        compiler_params=pltpu.CompilerParams(vmem_limit_bytes=24 * 1024 * 1024),
    )(coef_sin, coef_cos, weights)


def fourier_matrix(orders, longitudes):
    phases = (np.arange(orders)[:, None] * np.arange(longitudes)[None, :]) % longitudes
    angles = 2.0 * np.pi * phases / longitudes
    return np.stack([np.cos(angles), -np.sin(angles)]).astype(np.float32)


def body(grid_field, norm_gain, filter_weight):
    device_index = lax.axis_index("lat")
    lat_count = lax.axis_size("lat")
    band_rows, longitudes, columns = grid_field.shape
    total_lat = band_rows * lat_count
    order_count = DEG_DEV * lat_count
    all_rows = jnp.arange(total_lat, dtype=jnp.int32)
    colat_all = math.pi * (all_rows.astype(jnp.float32) + 0.5) / total_lat
    sine_all = jnp.sin(colat_all)
    own_rows = device_index * band_rows + jnp.arange(band_rows, dtype=jnp.int32)
    sine_own = jnp.sin(math.pi * (own_rows.astype(jnp.float32) + 0.5) / total_lat)

    first = jnp.einsum("j,jnx->x", sine_own, grid_field, precision=lax.Precision.HIGHEST)
    second = jnp.einsum(
        "j,jnx->x", sine_own, grid_field * grid_field, precision=lax.Precision.HIGHEST
    )
    band_mean = first / (longitudes * jnp.sum(sine_own))
    denominator_rows = jnp.float32(longitudes)
    cos_table, sin_table = fourier_matrix(order_count, longitudes)

    def transform(table):
        return jnp.einsum(
            "mn,jnx->mjx", jnp.asarray(table), grid_field, precision=lax.Precision.HIGH
        )

    def to_orders(raw):
        return lax.all_to_all(
            raw.astype(jnp.bfloat16), "lat", split_axis=0, concat_axis=1, tiled=True
        )

    def to_degrees(sums):
        return lax.all_to_all(
            sums, "lat", split_axis=0, concat_axis=0
        )

    received_sin = to_orders(transform(sin_table))
    constant = jnp.arange(order_count) == 0
    shift = jnp.where(constant[:, None, None], denominator_rows * band_mean, 0.0)
    received_cos = to_orders(transform(cos_table) - shift)

    weight_scale = math.pi**1.5 / math.sqrt(total_lat * longitudes)
    legendre = legendre_table(colat_all, device_index * DEG_DEV, order_count, weight_scale)

    def analyse(received):
        return jnp.einsum("mlj,mjx->mlx", legendre, received, preferred_element_type=jnp.float32)

    def by_degree(sums):
        ordered = sums.astype(jnp.bfloat16).transpose(1, 0, 2)
        return ordered.reshape(lat_count, DEG_DEV, DEG_DEV, columns)

    sums_sin = by_degree(analyse(received_sin))
    moments, sums_sin = lax.optimization_barrier(
        (jnp.stack([first, second, band_mean]), sums_sin)
    )
    gathered, sums_sin = lax.optimization_barrier((lax.all_gather(moments, "lat"), sums_sin))
    denominator = longitudes * jnp.sum(sine_all)
    average = jnp.sum(gathered[:, 0], axis=0) / denominator
    mean_square = jnp.sum(gathered[:, 1], axis=0) / denominator
    spread = jnp.sqrt(mean_square - average * average + 1e-05)
    factor = jnp.tile(norm_gain, S) / spread
    coef_sin = to_degrees(sums_sin)
    band_sums = jnp.sum(
        legendre[0].astype(jnp.float32).reshape(order_count, lat_count, band_rows), axis=2
    )
    level = jnp.dot(
        band_sums,
        denominator_rows * (gathered[:, 2] - average),
        precision=lax.Precision.HIGHEST,
    )
    here = (device_index == 0) & (jnp.arange(DEG_DEV) == 0)
    coef_cos = to_degrees(
        by_degree(analyse(received_cos) + jnp.where(here[:, None, None], level[None], 0.0))
    )

    expanded = expand_filter(filter_weight)
    expanded = (expanded * jnp.tile(factor, 2)[None, :, None]).astype(jnp.bfloat16)

    return mix(coef_sin, coef_cos, expanded)


def solution(mesh):
    in_specs = (P("lat", None, "parts"), P("parts"), P("lat", None, None, "parts"))
    out_specs = P("lat", None, "parts")
    return jax.shard_map(body, mesh=mesh, in_specs=in_specs, out_specs=out_specs, check_vma=False)
```

profile of v0, /device:TPU:29, one launch (start us, length us, event | category | flops | bytes accessed | tf_op | source)
XLA Modules:
  0.0 257.3 jit_solution(3099734840731700369)
XLA Ops:
  0.0 15.5 %convolution_convert_fusion = bf16[352,23,128]{2,0,1:T(8,128)(2,1)S(1)} fusion(f32[352,1440,1]{1,0,2:T(8,128)} %constant.113, f32[23,1440,128]{2,1,0:T(8,128)} %param.5), kind=kOutput, calls=%fused_computation.6 | convolution fusion | flops 8954564608 | bytes 21057536 | tf_op jit(solution)/shard_map/mn,jnx->mjx/dot_general | solution.py:193
  15.5 2.2 copy.19
  17.7 6.3 %all-to-all-start = ((bf16[352,23,128]{2,1,0:T(8,128)(2,1)}), bf16[352,23,128]{2,1,0:T(8,128)(2,1)S(1)}, u32[]{:S(2)}, u32[]{:S(2)}) async-start(bf16[352,23,128]{2,1,0:T(8,128)(2,1)} %copy.19), calls=%async_computation | async-start | bytes 4325376 | tf_op jit(solution)/shard_map/all_to_all | solution.py:198
  24.0 0.7 fusion.19
  25.4 7.5 %multiply_reduce_fusion = (f32[23,128]{1,0:T(8,128)S(1)}, f32[23,128]{1,0:T(8,128)S(1)}) fusion(f32[23,1440,128]{2,1,0:T(8,128)} %param.5), kind=kLoop, calls=%fused_computation | loop fusion | flops 12712192 | bytes 16980992 | tf_op jit(solution)/shard_map/j,jnx->x/reduce_sum | solution.py:185
  32.9 0.2 broadcast_multiply_fusion
  33.1 0.1 broadcast_select_fusion
  33.2 15.6 %subtract_convert_fusion = bf16[352,23,128]{2,0,1:T(8,128)(2,1)S(1)} fusion(f32[352,128]{1,0:T(8,128)S(1)} %broadcast_select_fusion, f32[352,1440,1]{1,0,2:T(8,128)} %constant.114, f32[23,1440,128]{2,1,0:T(8,128)} %param.5), kind=kOutput, calls=%fused_computation.2 | convolution fusion | flops 8955600896 | bytes 21237760 | tf_op jit(solution)/shard_map/mn,jnx->mjx/dot_general | solution.py:193
  48.8 2.2 copy.22
  50.9 21.0 %all-to-all-done = bf16[352,23,128]{2,1,0:T(8,128)(2,1)S(1)} async-done(((bf16[352,23,128]{2,1,0:T(8,128)(2,1)}), bf16[352,23,128]{2,1,0:T(8,128)(2,1)S(1)}, u32[]{:S(2)}, u32[]{:S(2)}) %all-to-all-start) | async-done | bytes 2072608 | tf_op jit(solution)/shard_map/all_to_all | solution.py:198
  71.9 1.3 copy-done.4
  73.2 5.9 %all-to-all-start.2 = ((bf16[352,23,128]{2,1,0:T(8,128)(2,1)}), bf16[352,23,128]{2,1,0:T(8,128)(2,1)S(1)}, u32[]{:S(2)}, u32[]{:S(2)}) async-start(bf16[352,23,128]{2,1,0:T(8,128)(2,1)} %copy.22), calls=%async_computation.2 | async-start | bytes 4325376 | tf_op jit(solution)/shard_map/all_to_all | solution.py:198
  79.2 0.1 add_multiply_fusion.1
  79.3 0.2 fusion.15
  79.5 0.1 fusion.1
  79.6 15.5 %shard_map.55 = bf16[22,352,368]{2,1,0:T(8,128)(2,1)S(1)} custom-call(f32[24,384]{1,0:T(8,128)S(1)} %broadcast_in_dim.57.orders_ref, f32[1,384]{1,0:T(1,128)S(1)} %broadcast_in_dim.58.cosine_ref, f32[1,384]{1,0:T(1,128)S(1)} %broadcast_in_dim.59.weights_ref, f32[24,384]{1,0:T(8,128)S(1)} %get-tuple-element.25.mant_ref, f32[24,384]{1,0:T(8,128)S(1)} %get-tuple-element.24.exp_ref), custom_call_target="tpu_custom_call" | custom-call | flops 6488064000 | bytes 5699584 | tf_op jit(solution)/shard_map/pallas_call | solution.py:98
  95.1 2.5 copy-done.2
  97.7 1.9 copy.20
  99.6 4.1 %all_to_all.35 = bf16[22,368,128]{2,1,0:T(8,128)(2,1)} reshape(bf16[22,16,23,128]{3,2,1,0:T(8,128)(2,1)} %copy.20) | data formatting | bytes 4145152 | tf_op jit(solution)/shard_map/all_to_all | solution.py:198
  103.7 5.0 %convert_bitcast_fusion = bf16[352,22,128]{2,0,1:T(8,128)(2,1)S(1)} fusion(bf16[22,352,368]{2,1,0:T(8,128)(2,1)} %copy-done.2, bf16[22,368,128]{2,1,0:T(8,128)(2,1)} %all_to_all.35), kind=kOutput, calls=%fused_computation.5 | convolution fusion | flops 730537984 | bytes 9754624 | tf_op jit(solution)/shard_map/mlj,mjx->mlx/dot_general | solution.py:216
  108.7 2.1 copy.21
  110.9 25.6 %all-gather.1 = f32[16,3,128]{2,1,0:T(4,128)S(1)} all-gather(f32[1,3,128]{2,1,0:T(4,128)S(1)} %bitcast.57), channel_id=2, replica_groups=mesh['parts'=2,'lat'=16] {'lat'}, dimensions={0}, use_global_device_ids=true | all-gather | bytes 26112 | tf_op jit(solution)/shard_map/all_gather | solution.py:226
  136.5 1.3 copy-done.3
  137.8 5.9 %all-to-all-start.1 = ((bf16[16,22,22,128]{3,2,1,0:T(8,128)(2,1)}), bf16[16,22,22,128]{3,2,1,0:T(8,128)(2,1)S(1)}, u32[]{:S(2)}, u32[]{:S(2)}) async-start(bf16[16,22,22,128]{3,2,1,0:T(8,128)(2,1)} %bitcast.53), calls=%async_computation.1 | async-start | bytes 4325376 | tf_op jit(solution)/shard_map/all_to_all | solution.py:203
  143.7 1.0 slice_convert_fusion
  144.7 0.2 copy.24
  145.0 0.1 tile.7
  145.1 0.7 sine_reduce_fusion
  146.5 0.1 reduce_sum.66
  146.6 3.6 %copy.23 = bf16[22,16,23,128]{3,2,1,0:T(8,128)(2,1)} copy(bf16[22,16,23,128]{3,2,0,1:T(8,128)(2,1)} %bitcast.51) | data formatting | bytes 4145152 | tf_op jit(solution)/shard_map/all_to_all | solution.py:198
  150.2 4.1 %all_to_all.40 = bf16[22,368,128]{2,1,0:T(8,128)(2,1)} reshape(bf16[22,16,23,128]{3,2,1,0:T(8,128)(2,1)} %copy.23) | data formatting | bytes 4145152 | tf_op jit(solution)/shard_map/all_to_all | solution.py:198
  154.3 0.5 fusion.2
  154.8 5.1 %fusion = bf16[352,22,128]{2,0,1:T(8,128)(2,1)S(1)} fusion(bf16[22,352,368]{2,1,0:T(8,128)(2,1)} %copy-done.2, bf16[22,368,128]{2,1,0:T(8,128)(2,1)} %all_to_all.40, f32[352,128]{1,0:T(8,128)S(1)} %fusion.2, pred[22]{0:T(512)(128)(4,1)S(1)} %compare_and_fusion), kind=kOutput, calls=%fused_computation.4 | convolution fusion | flops 732520448 | bytes 9934870 | tf_op jit(solution)/shard_map/mlj,mjx->mlx/dot_general | solution.py:216
  159.9 2.1 copy.25
  162.0 29.5 %all-to-all-done.1.sin_ref = bf16[16,22,22,128]{3,2,1,0:T(8,128)(2,1)S(1)} async-done(((bf16[16,22,22,128]{3,2,1,0:T(8,128)(2,1)}), bf16[16,22,22,128]{3,2,1,0:T(8,128)(2,1)S(1)}, u32[]{:S(2)}, u32[]{:S(2)}) %all-to-all-start.1) | async-done | bytes 1982496 | tf_op jit(solution)/shard_map/all_to_all | solution.py:203
  191.6 1.4 copy-done
  193.0 5.9 %all-to-all-start.3 = ((bf16[16,22,22,128]{3,2,1,0:T(8,128)(2,1)}), bf16[16,22,22,128]{3,2,1,0:T(8,128)(2,1)}, u32[]{:S(2)}, u32[]{:S(2)}) async-start(bf16[16,22,22,128]{3,2,1,0:T(8,128)(2,1)} %bitcast.54), calls=%async_computation.3 | async-start | bytes 4325376 | tf_op jit(solution)/shard_map/all_to_all | solution.py:203
  198.9 0.1 maximum_bitcast_fusion.1
  199.1 0.3 maximum_bitcast_fusion
  199.4 1.5 copy.26
  200.9 5.0 %mul.126 = bf16[22,2,2,64,2,2,64]{6,5,4,3,2,1,0:T(2,128)(2,1)} broadcast(bf16[22,2,64,2,64]{4,3,2,1,0:T(2,128)(2,1)S(1)} %copy.26), dimensions={0,1,3,4,6} | broadcast | bytes 3604480 | tf_op jit(solution)/shard_map/mul | solution.py:132
  205.9 11.2 %mul.127 = bf16[22,256,256]{2,1,0:T(8,128)(2,1)} reshape(bf16[22,2,2,64,2,2,64]{6,5,4,3,2,1,0:T(2,128)(2,1)} %mul.126) | data formatting | bytes 5767168 | tf_op jit(solution)/shard_map/mul | solution.py:132
  217.1 0.2 mul.128
  217.3 0.2 mul.129
  217.6 2.6 %multiply_convert_fusion.weight_ref = bf16[22,256,256]{2,1,0:T(8,128)(2,1)S(1)} fusion(f32[256]{0:T(256)S(1)} %broadcast_bitcast_fusion, bf16[22,256,256]{2,1,0:T(8,128)(2,1)} %mul.127, bf16[256,256]{1,0:T(8,128)(2,1)S(1)} %mul.129), kind=kLoop, calls=%fused_computation.1 | loop fusion | flops 5767168 | bytes 5899264 | tf_op jit(solution)/shard_map/convert_element_type | solution.py:247
  220.2 26.6 %all-to-all-done.3.cos_ref = bf16[16,22,22,128]{3,2,1,0:T(8,128)(2,1)} async-done(((bf16[16,22,22,128]{3,2,1,0:T(8,128)(2,1)}), bf16[16,22,22,128]{3,2,1,0:T(8,128)(2,1)}, u32[]{:S(2)}, u32[]{:S(2)}) %all-to-all-start.3) | async-done | bytes 1982496 | tf_op jit(solution)/shard_map/all_to_all | solution.py:203
  246.8 1.6 copy-done.1
  248.4 8.9 %shard_map.56 = bf16[22,352,256]{2,1,0:T(8,128)(2,1)} custom-call(bf16[16,22,22,128]{3,2,1,0:T(8,128)(2,1)S(1)} %copy-done.1, bf16[16,22,22,128]{3,2,1,0:T(8,128)(2,1)} %all-to-all-done.3.cos_ref, bf16[22,256,256]{2,1,0:T(8,128)(2,1)S(1)} %multiply_convert_fusion.weight_ref), custom_call_target="tpu_custom_call" | custom-call | tf_op jit(solution)/shard_map/pallas_call | solution.py:155
  (28 shorter events, 0.4 us)
Async XLA Ops:
  17.7 54.2 %all-to-all-start = ((bf16[352,23,128]{2,1,0:T(8,128)(2,1)}), bf16[352,23,128]{2,1,0:T(8,128)(2,1)S(1)}, u32[]{:S(2)}, u32[]{:S(2)}) async-start(bf16[352,23,128]{2,1,0:T(8,128)(2,1)} %copy.19), calls=%async_computation | async-start | bytes 4325376 | tf_op jit(solution)/shard_map/all_to_all | solution.py:198
  71.9 1.3 copy-start.4
  73.2 63.3 %all-to-all-start.2 = ((bf16[352,23,128]{2,1,0:T(8,128)(2,1)}), bf16[352,23,128]{2,1,0:T(8,128)(2,1)S(1)}, u32[]{:S(2)}, u32[]{:S(2)}) async-start(bf16[352,23,128]{2,1,0:T(8,128)(2,1)} %copy.22), calls=%async_computation.2 | async-start | bytes 4325376 | tf_op jit(solution)/shard_map/all_to_all | solution.py:198
  79.6 18.0 %copy-start.5 = (bf16[352,23,128]{2,1,0:T(8,128)(2,1)S(1)}, bf16[352,23,128]{2,1,0:T(8,128)(2,1)}, u32[]{:S(2)}) copy-start(bf16[352,23,128]{2,1,0:T(8,128)(2,1)} %copy-done.4) | copy-start | bytes 6217732
  95.1 2.5 copy-start.2
  136.5 1.3 copy-start.3
  137.8 53.7 %all-to-all-start.1 = ((bf16[16,22,22,128]{3,2,1,0:T(8,128)(2,1)}), bf16[16,22,22,128]{3,2,1,0:T(8,128)(2,1)S(1)}, u32[]{:S(2)}, u32[]{:S(2)}) async-start(bf16[16,22,22,128]{3,2,1,0:T(8,128)(2,1)} %bitcast.53), calls=%async_computation.1 | async-start | bytes 4325376 | tf_op jit(solution)/shard_map/all_to_all | solution.py:203
  143.7 1.3 copy-start.7
  191.6 1.4 copy-start
  191.6 7.3 %copy-start.6 = (bf16[22,2,64,64]{3,2,1,0:T(8,128)(2,1)S(1)}, bf16[22,2,64,64]{3,2,1,0:T(8,128)(2,1)}, u32[]{:S(2)}) copy-start(bf16[22,2,64,64]{3,2,1,0:T(8,128)(2,1)} %param.7) | copy-start | bytes 1081348
  193.0 53.8 %all-to-all-start.3 = ((bf16[16,22,22,128]{3,2,1,0:T(8,128)(2,1)}), bf16[16,22,22,128]{3,2,1,0:T(8,128)(2,1)}, u32[]{:S(2)}, u32[]{:S(2)}) async-start(bf16[16,22,22,128]{3,2,1,0:T(8,128)(2,1)} %bitcast.54), calls=%async_computation.3 | async-start | bytes 4325376 | tf_op jit(solution)/shard_map/all_to_all | solution.py:203
  246.8 1.6 copy-start.1
where the time goes:
time: 260 us; the launch traced here: 257 us
  waiting for transfers between devices  77.1 us (30%)
  local copies, waits for them, and re-layouts  49.1 us (19%)
  matrix products  42 us (16%)
  blocking collectives  25.6 us (10%)
  Pallas kernels  24.3 us (9%)
  starting transfers between devices  23.9 us (9%)
  other arithmetic  13.6 us (5%)
    all_to_all x2, waiting for transfers between devices, to_degrees(): return lax.all_to_all(sums, 'lat', split_axis=0, concat_axis=0)  56.2 us
    dot_general x2, matrix products, transform(): jnp.einsum('mn,jnx->mjx', jnp.asarray(table), grid_field, precision=lax.P...  31.1 us
    all_gather x1, blocking collectives, body(): lax.all_gather(moments, 'lat')  25.6 us
    all_to_all x2, waiting for transfers between devices, to_orders(): lax.all_to_all(raw.astype(jnp.bfloat16), 'lat', split_axis=0, concat_axis...  21 us
    mul x4, local copies, waits for them, and re-layouts, expand_filter(): mixing.transpose(0, 1, 3, 2, 4)[:, :, None, :, :, None, :]  16.6 us
    pallas_call x1, Pallas kernels, legendre_table(): pl.pallas_call(legendre_kernel, grid=(degrees // BLOCK,), out_shape=jax.S...  15.5 us
    all_to_all x4, local copies, waits for them, and re-layouts, to_orders(): lax.all_to_all(raw.astype(jnp.bfloat16), 'lat', split_axis=0, concat_axis...  13.7 us
    all_to_all x2, starting transfers between devices, to_orders(): lax.all_to_all(raw.astype(jnp.bfloat16), 'lat', split_axis=0, concat_axis...  12.2 us
  transfers between devices with their start and end apart: 4, of which 3 were waited for; matrix products, arithmetic and copies ran while one was open for 27% of the time, Pallas kernels for 6%

commit v1 on v0

--- a/solution.py
+++ b/solution.py
@@ -1,3 +1,4 @@
+import functools
 import math
 
 import jax
@@ -169,7 +170,7 @@
     return np.stack([np.cos(angles), -np.sin(angles)]).astype(np.float32)
 
 
-def body(grid_field, norm_gain, filter_weight):
+def plain_body(grid_field, norm_gain, filter_weight):
     device_index = lax.axis_index("lat")
     lat_count = lax.axis_size("lat")
     band_rows, longitudes, columns = grid_field.shape
@@ -249,6 +250,643 @@
     return mix(coef_sin, coef_cos, expanded)
 
 
+MESH = pl.DeviceIdType.MESH
+ROWS = 8
+WIDE = 2 * LANES
+CHUNKS = 3
+PLANE = 4
+PLANE_CHUNKS = PLANE * CHUNKS - 1
+VMEM_CAP = 60 * 1024 * 1024
+
+
+def owner_rank(device):
+    plane, inner = device // PLANE, device % PLANE
+    flip = (inner // 2 + plane) % 2
+    core = inner % 2
+    return flip * (1 + core) + (1 - flip) * (PLANE - 1) * core
+
+
+def owner_chunk(device, slot, count):
+    plane = device // PLANE
+    base = PLANE_CHUNKS * (count // PLANE - 1 - plane)
+    return base + PLANE_CHUNKS - 1 - PLANE * slot - owner_rank(device)
+
+
+def transform_tables(count, longitudes):
+    table = np.zeros((CHUNKS, 2, count, ROWS, longitudes), np.float64)
+    for slot in range(CHUNKS):
+        for device in range(count):
+            if slot == CHUNKS - 1 and owner_rank(device) == PLANE - 1:
+                continue
+            orders = owner_chunk(device, slot, count) * ROWS + np.arange(ROWS)
+            phases = (orders[:, None] * np.arange(longitudes)[None, :]) % longitudes
+            angles = 2.0 * np.pi * phases / longitudes
+            table[slot, 0, device] = np.cos(angles)
+            table[slot, 1, device] = -np.sin(angles)
+    table = table.reshape(CHUNKS, 2 * count * ROWS, longitudes).astype(np.float32)
+    high = table.astype(jnp.bfloat16)
+    low = (table - high.astype(np.float32)).astype(jnp.bfloat16)
+    return high, low
+
+
+def angle_tables(count, band, places):
+    colat = np.pi * (np.arange(count * band) + 0.5) / (count * band)
+    by_place = np.full((count, places), 0.5 * np.pi)
+    valid = np.zeros((count, places))
+    for device in range(count):
+        rows = colat[device * band : (device + 1) * band]
+        by_place[device, :band] = rows if device < count // 2 else rows[::-1]
+        valid[device, :band] = 1.0
+    sine_places = np.sin(by_place) * valid
+    north = by_place[: count // 2].reshape(1, -1)
+    weight = sine_places[: count // 2].reshape(1, -1)
+    width = round_up(north.shape[1], LANES)
+    north = np.pad(north, ((0, 0), (0, width - north.shape[1])), constant_values=0.5 * np.pi)
+    weight = np.pad(weight, ((0, 0), (0, width - weight.shape[1])))
+    return (
+        sine_places.reshape(-1).astype(np.float32),
+        np.cos(north).astype(np.float32),
+        weight,
+        np.log(np.sin(north)).astype(np.float32),
+        float(np.sum(np.sin(colat))),
+    )
+
+
+def log_starts(order_count):
+    values = [
+        0.5 * math.log((2.0 * m + 1.0) / (4.0 * math.pi))
+        + 0.5 * (math.lgamma(m + 0.5) - math.lgamma(m + 1.0) - 0.5 * math.log(math.pi))
+        for m in range(order_count)
+    ]
+    return np.broadcast_to(np.asarray(values, np.float32)[:, None], (order_count, LANES))
+
+
+def spectral_kernel(
+    sizes,
+    field_ref,
+    gain_ref,
+    high_ref,
+    low_ref,
+    sine_ref,
+    cosine_ref,
+    weight_ref,
+    logsine_ref,
+    start_ref,
+    out_ref,
+    high,
+    low,
+    stage,
+    field_high,
+    field_low,
+    turned,
+    outgoing,
+    landed,
+    moments,
+    moments_all,
+    scales,
+    table,
+    prev_ref,
+    early_ref,
+    grow_ref,
+    mant_ref,
+    exp_ref,
+    lines,
+    sums,
+    sums_out,
+    table_sem,
+    stage_sem,
+    moment_send,
+    moment_recv,
+    send_sem,
+    recv_sem,
+    local_sem,
+    send_two,
+    recv_two,
+):
+    count, band, longitudes, total_sine = sizes
+    me = lax.axis_index("lat")
+    part = lax.axis_index("parts")
+    half = count // 2
+    south = me // half
+    slot_of_me = me + south * (half + count - 1 - 2 * me)
+    groups = outgoing.shape[0] // CHUNKS
+    places = groups * ROWS
+    degrees = table.shape[1]
+    kept = table.shape[2]
+    width = cosine_ref.shape[1]
+    block_rows = DEG_DEV * ROWS
+    zero_owner = [
+        d for d in range(count) if owner_chunk(d, CHUNKS - 1, count) == 0 and owner_rank(d) < PLANE - 1
+    ][0]
+    has_last = owner_rank(me) < PLANE - 1
+
+    def has_chunk(slot, device):
+        return (slot < CHUNKS - 1) | (owner_rank(device) < PLANE - 1)
+
+    def table_copies(slot):
+        return (
+            pltpu.make_async_copy(high_ref.at[slot], high.at[slot], table_sem.at[0, slot]),
+            pltpu.make_async_copy(low_ref.at[slot], low.at[slot], table_sem.at[1, slot]),
+        )
+
+    def row_copy(place):
+        row = place + south * (band - 1 - 2 * place)
+        at = place % ROWS
+        return pltpu.make_async_copy(field_ref.at[row], stage.at[at], stage_sem.at[at])
+
+    for place in range(2):
+        row_copy(place).start()
+    for copy in table_copies(0):
+        copy.start()
+    for place in range(2, ROWS):
+        row_copy(place).start()
+    for slot in range(1, CHUNKS):
+        for copy in table_copies(slot):
+            copy.start()
+
+    barrier = pltpu.get_barrier_semaphore()
+
+    @pl.loop(1, count)
+    def _(step):
+        pl.semaphore_signal(
+            barrier, inc=1, device_id=(part, (me + step) % count), device_id_type=MESH
+        )
+
+    moments[...] = jnp.zeros_like(moments)
+    for place in range(band, places):
+        lanes = slice((place % 2) * LANES, (place % 2 + 1) * LANES)
+        field_high[place // 2, :, lanes] = jnp.zeros((longitudes, LANES), jnp.bfloat16)
+        field_low[place // 2, :, lanes] = jnp.zeros((longitudes, LANES), jnp.bfloat16)
+
+    piece = longitudes // 6
+
+    def take_row(place, lanes):
+        row_copy(place).wait()
+        at = place % ROWS
+        pair = place // 2
+        total = jnp.zeros((ROWS, LANES), jnp.float32)
+        square = jnp.zeros((ROWS, LANES), jnp.float32)
+        for first in range(0, longitudes, piece):
+            value = stage[at, first : first + piece, :]
+            top = value.astype(jnp.bfloat16)
+            field_high[pair, first : first + piece, lanes] = top
+            field_low[pair, first : first + piece, lanes] = (
+                value - top.astype(jnp.float32)
+            ).astype(jnp.bfloat16)
+            total += jnp.sum(value.reshape(-1, ROWS, LANES), axis=0)
+            square += jnp.sum((value * value).reshape(-1, ROWS, LANES), axis=0)
+        sine = sine_ref[me * places + place]
+        moments[:ROWS] += sine * total
+        moments[ROWS:] += sine * square
+
+        @pl.when(place + ROWS < band)
+        def _():
+            row_copy(place + ROWS).start()
+
+    def take_group(group):
+        @pl.loop(0, ROWS // 2)
+        def _(pair):
+            place = group * ROWS + 2 * pair
+            take_row(place, slice(0, LANES))
+
+            @pl.when(place + 1 < band)
+            def _():
+                take_row(place + 1, slice(LANES, WIDE))
+
+    take_group(0)
+    pl.semaphore_wait(barrier, count - 1)
+
+    def moment_copy(device):
+        return pltpu.make_async_remote_copy(
+            moments,
+            moments_all.at[me],
+            moment_send,
+            moment_recv,
+            device_id=(part, device),
+            device_id_type=MESH,
+        )
+
+    def order_copy(slot, group, device):
+        step = slot * groups + group
+        rows = pl.ds(pl.multiple_of(device * ROWS * ROWS, ROWS * ROWS), ROWS * ROWS)
+        return pltpu.make_async_remote_copy(
+            outgoing.at[step, rows],
+            landed.at[slot, slot_of_me, group],
+            send_sem.at[step],
+            recv_sem.at[slot],
+            device_id=(part, device),
+            device_id_type=MESH,
+        )
+
+    def own_copy(slot, group):
+        step = slot * groups + group
+        rows = pl.ds(pl.multiple_of(me * ROWS * ROWS, ROWS * ROWS), ROWS * ROWS)
+        return pltpu.make_async_copy(
+            outgoing.at[step, rows], landed.at[slot, slot_of_me, group], local_sem.at[step]
+        )
+
+    @pl.loop(0, CHUNKS * groups)
+    def _(step):
+        slot, group = step // groups, step % groups
+
+        @pl.when((step > 0) & (slot == 0))
+        def _():
+            take_group(group)
+
+        @pl.when(step == groups - 1)
+        def _():
+            moments_all[me] = moments[...]
+
+            @pl.loop(1, count)
+            def _(ahead):
+                moment_copy((me + ahead) % count).start()
+
+        @pl.when(group == 0)
+        def _():
+            for copy in table_copies(slot):
+                copy.wait()
+
+        @pl.when(step == (CHUNKS - 1) * groups)
+        def _():
+            pltpu.make_async_copy(
+                moments_all.at[pl.ds(0, count - 1)],
+                moments_all.at[pl.ds(0, count - 1)],
+                moment_recv,
+            ).wait()
+            gathered = jnp.sum(moments_all[...], axis=0)
+            first = jnp.sum(gathered[:ROWS], axis=0, keepdims=True) / (longitudes * total_sine)
+            second = jnp.sum(gathered[ROWS:], axis=0, keepdims=True) / (longitudes * total_sine)
+            spread = jnp.sqrt(second - first * first + 1e-05)
+            gain = gain_ref[...]
+            factor = jnp.concatenate([gain] * S, axis=1) / spread
+            scales[:1] = jnp.concatenate([factor, factor], axis=1)
+            scales[1:2] = jnp.concatenate([longitudes * first, jnp.zeros_like(first)], axis=1)
+
+        @pl.loop(0, ROWS // 2)
+        def _(pair):
+            at = group * (ROWS // 2) + pair
+            product = jnp.dot(high[slot], field_high[at], preferred_element_type=jnp.float32)
+            product += jnp.dot(high[slot], field_low[at], preferred_element_type=jnp.float32)
+            product += jnp.dot(low[slot], field_high[at], preferred_element_type=jnp.float32)
+            lines_of = count * ROWS
+            for side in range(2):
+                for row in range(2):
+                    turned[side, pl.ds(2 * pair + row, lines_of, stride=ROWS), :] = product[
+                        side * lines_of : (side + 1) * lines_of, row * LANES : (row + 1) * LANES
+                    ]
+
+        @pl.when(slot == CHUNKS - 1)
+        def _():
+            at = zero_owner * ROWS * ROWS
+            turned[0, at : at + ROWS, :] -= scales[1:2, :LANES]
+
+        @pl.loop(0, count)
+        def _(ahead):
+            device = (me + 1 + ahead) % count
+            rows = pl.ds(pl.multiple_of(device * ROWS * ROWS, ROWS * ROWS), ROWS * ROWS)
+            outgoing[step, rows, :] = jnp.concatenate(
+                [turned[0, rows, :], turned[1, rows, :]], axis=1
+            ).astype(jnp.bfloat16)
+
+            @pl.when((device != me) & has_chunk(slot, device))
+            def _():
+                order_copy(slot, group, device).start()
+
+            @pl.when((device == me) & has_chunk(slot, device))
+            def _():
+                own_copy(slot, group).start()
+
+    chunk_of = [owner_chunk(me, slot, count) for slot in range(CHUNKS)]
+    chunk_of[-1] = jnp.maximum(chunk_of[-1], 0)
+    lines_in = lax.broadcasted_iota(jnp.int32, (ROWS, width), 0)
+    orders = jnp.concatenate(
+        [(chunk * ROWS + lines_in).astype(jnp.float32) for chunk in chunk_of], axis=0
+    )
+    start = jnp.concatenate(
+        [start_ref[pl.ds(pl.multiple_of(chunk * ROWS, ROWS), ROWS), :] for chunk in chunk_of], axis=0
+    )
+
+    def widen(value):
+        return jnp.concatenate([value] * (width // LANES), axis=1)
+
+    log_diag = widen(start) + orders * logsine_ref[...]
+    start_exp = 64.0 * jnp.floor(log_diag / (64.0 * math.log(2.0)))
+    exp_ref[...] = start_exp
+    mant_ref[...] = jnp.exp(log_diag - start_exp * math.log(2.0))
+    prev_ref[...] = jnp.zeros_like(prev_ref)
+    early_ref[...] = jnp.zeros_like(early_ref)
+    grow_ref[...] = jnp.zeros_like(grow_ref)
+    order_lines = CHUNKS * ROWS
+
+    @pl.loop(0, degrees // BLOCK)
+    def _(block):
+        narrow = orders[:, :LANES]
+        order_sq = narrow * narrow
+        cosine = cosine_ref[...]
+        weights = weight_ref[...]
+        limit = 2.0**64
+        shrink = 2.0 ** (-64)
+        previous, earlier, exponent = prev_ref[...], early_ref[...], grow_ref[...]
+        first = (block * BLOCK).astype(jnp.float32)
+        for step in range(BLOCK):
+            degree = first + float(step)
+            upper = jnp.sqrt(
+                (4.0 * degree * degree - 1.0) / jnp.maximum(degree * degree - order_sq, 1.0)
+            )
+            below = degree - 1.0
+            lower = jnp.sqrt(
+                jnp.maximum(below * below - order_sq, 0.0)
+                / jnp.maximum(jnp.full_like(order_sq, 4.0 * below * below - 1.0), 1.0)
+            )
+            recurred = widen(upper) * (cosine * previous - widen(lower) * earlier)
+            at_start = orders == degree
+            current = jnp.where(at_start, mant_ref[...], jnp.where(orders < degree, recurred, 0.0))
+            exponent = jnp.where(at_start, exp_ref[...], exponent)
+            value = weights * (current * jnp.exp2(exponent))
+            for lane in range(width // LANES):
+                lines[lane, step * order_lines : (step + 1) * order_lines, :] = value[
+                    :, lane * LANES : (lane + 1) * LANES
+                ]
+            large = jnp.abs(current) > limit
+            earlier = jnp.where(large, previous * shrink, previous)
+            previous = jnp.where(large, current * shrink, current)
+            exponent = jnp.where(large, exponent + 64.0, exponent)
+        prev_ref[...] = previous
+        early_ref[...] = earlier
+        grow_ref[...] = exponent
+        rows = pl.ds(pl.multiple_of(block * BLOCK, BLOCK), BLOCK)
+        for order in range(order_lines):
+            for lane in range(0, width, LANES):
+                cut = min(LANES, kept - lane)
+                part_of = lines[lane // LANES, pl.ds(order, BLOCK, stride=order_lines), :]
+                table[order, rows, lane : lane + cut] = part_of[:, :cut].astype(table.dtype)
+
+    def reaches(chunk, device):
+        return chunk * ROWS <= device * DEG_DEV + DEG_DEV - 1
+
+    def degree_copy(slot, device):
+        chunk = owner_chunk(me, slot, count)
+        rows = pl.ds(pl.multiple_of(device * block_rows, block_rows), block_rows)
+        return pltpu.make_async_remote_copy(
+            sums_out.at[slot, rows],
+            out_ref.at[chunk],
+            send_two.at[slot, device],
+            recv_two.at[chunk],
+            device_id=(part, device),
+            device_id_type=MESH,
+        )
+
+    def own_degrees(slot):
+        chunk = owner_chunk(me, slot, count)
+        rows = pl.ds(pl.multiple_of(me * block_rows, block_rows), block_rows)
+        return pltpu.make_async_copy(sums_out.at[slot, rows], out_ref.at[chunk], recv_two.at[chunk])
+
+    degree_line = lax.broadcasted_iota(jnp.int32, (degrees, 1), 0)
+    sign_even = jnp.where(degree_line % 2 == 0, 1.0, -1.0).astype(jnp.float32)
+
+    def analyse(slot):
+        pltpu.make_async_copy(
+            landed.at[slot, pl.ds(0, count - 1)],
+            landed.at[slot, pl.ds(0, count - 1)],
+            recv_sem.at[slot],
+        ).wait()
+        for group in range(groups):
+            own_copy(slot, group).wait()
+
+        @pl.loop(0, ROWS // 2)
+        def _(pair):
+            rows = pl.ds(pl.multiple_of(pair * 2 * ROWS, 2 * ROWS), 2 * ROWS)
+            both = landed[slot, :, :, rows, :].astype(jnp.float32)
+            both = both.reshape(count * groups, 2, ROWS, WIDE)
+            for odd in range(2):
+                rhs = both[:, odd].reshape(count * places, WIDE).astype(jnp.bfloat16)
+                lhs = table[slot * ROWS + 2 * pair + odd]
+                north = jnp.dot(lhs, rhs[:kept], preferred_element_type=jnp.float32)
+                mirror = jnp.dot(lhs, rhs[kept:], preferred_element_type=jnp.float32)
+                sign = sign_even if odd == 0 else -sign_even
+                result = (north + sign * mirror) * scales[:1]
+                for lane in range(2):
+                    sums[lane, pl.ds(2 * pair + odd, degrees, stride=ROWS), :] = result[
+                        :, lane * LANES : (lane + 1) * LANES
+                    ]
+
+        @pl.loop(0, count)
+        def _(ahead):
+            device = (me + 1 + ahead) % count
+            rows = pl.ds(pl.multiple_of(device * block_rows, block_rows), block_rows)
+            sums_out[slot, rows, :] = jnp.concatenate(
+                [sums[0, rows, :], sums[1, rows, :]], axis=1
+            ).astype(jnp.bfloat16)
+            wanted = reaches(owner_chunk(me, slot, count), device)
+
+            @pl.when(wanted & (device != me))
+            def _():
+                degree_copy(slot, device).start()
+
+            @pl.when(wanted & (device == me))
+            def _():
+                own_degrees(slot).start()
+
+    @pl.loop(0, CHUNKS)
+    def _(slot):
+        @pl.when((slot < CHUNKS - 1) | has_last)
+        def _():
+            analyse(slot)
+
+    pltpu.make_async_copy(
+        moments_all.at[pl.ds(0, count - 1)], moments_all.at[pl.ds(0, count - 1)], moment_send
+    ).wait()
+
+    def wait_orders(step, devices):
+        rows = pl.ds(0, devices * ROWS * ROWS)
+        pltpu.make_async_copy(
+            outgoing.at[step, rows], outgoing.at[step, rows], send_sem.at[step]
+        ).wait()
+
+    @pl.loop(0, (CHUNKS - 1) * groups)
+    def _(step):
+        wait_orders(step, count - 1)
+
+    last_owners = count - count // PLANE
+
+    @pl.loop((CHUNKS - 1) * groups, CHUNKS * groups)
+    def _(step):
+        @pl.when(has_last)
+        def _():
+            wait_orders(step, last_owners - 1)
+
+        @pl.when(jnp.logical_not(has_last))
+        def _():
+            wait_orders(step, last_owners)
+
+    @pl.loop(0, CHUNKS)
+    def _(slot):
+        @pl.loop(0, count)
+        def _(device):
+            wanted = reaches(owner_chunk(me, slot, count), device)
+
+            @pl.when(wanted & (device != me) & has_chunk(slot, me))
+            def _():
+                degree_copy(slot, device).wait_send()
+
+    @pl.loop(0, (me * DEG_DEV + DEG_DEV - 1) // ROWS + 1)
+    def _(chunk):
+        pltpu.make_async_copy(out_ref.at[chunk], out_ref.at[chunk], recv_two.at[chunk]).wait()
+
+
+def scratch_of(count, band, longitudes):
+    groups = -(-band // ROWS)
+    places = groups * ROWS
+    degrees = DEG_DEV * count
+    lines_of = count * ROWS
+    kept = count // 2 * places
+    width = round_up(kept, LANES)
+    order_lines = CHUNKS * ROWS
+    state = (order_lines, width)
+    bf16, f32 = jnp.bfloat16, jnp.float32
+    return [
+        ((CHUNKS, 2 * lines_of, longitudes), bf16),
+        ((CHUNKS, 2 * lines_of, longitudes), bf16),
+        ((ROWS, longitudes, LANES), f32),
+        ((places // 2, longitudes, WIDE), bf16),
+        ((places // 2, longitudes, WIDE), bf16),
+        ((2, lines_of * ROWS, LANES), f32),
+        ((CHUNKS * groups, lines_of * ROWS, WIDE), bf16),
+        ((CHUNKS, count, groups, ROWS * ROWS, WIDE), bf16),
+        ((2 * ROWS, LANES), f32),
+        ((count, 2 * ROWS, LANES), f32),
+        ((ROWS, WIDE), f32),
+        ((order_lines, degrees, kept), bf16),
+        (state, f32),
+        (state, f32),
+        (state, f32),
+        (state, f32),
+        (state, f32),
+        ((width // LANES, BLOCK * order_lines, LANES), f32),
+        ((2, degrees * ROWS, LANES), f32),
+        ((CHUNKS, degrees * ROWS, WIDE), bf16),
+    ]
+
+
+def scratch_bytes(shapes):
+    total = 0
+    for shape, dtype in shapes:
+        size = math.prod(shape[:-1]) * round_up(shape[-1], LANES)
+        total += size * jnp.dtype(dtype).itemsize
+    return total
+
+
+def coefficients_of(grid_field, norm_gain, count):
+    band, longitudes, columns = grid_field.shape
+    groups = -(-band // ROWS)
+    places = groups * ROWS
+    order_count = DEG_DEV * count
+    high, low = transform_tables(count, longitudes)
+    sine, cosine, weight, logsine, total_sine = angle_tables(count, band, places)
+    weight_scale = math.pi**1.5 / math.sqrt(count * band * longitudes)
+    shapes = scratch_of(count, band, longitudes)
+    dma = pltpu.SemaphoreType.DMA
+    vmem = pl.BlockSpec(memory_space=pltpu.VMEM)
+    anywhere = pl.BlockSpec(memory_space=pl.ANY)
+    return pl.pallas_call(
+        functools.partial(spectral_kernel, (count, band, longitudes, total_sine)),
+        out_shape=jax.ShapeDtypeStruct((order_count // ROWS, DEG_DEV * ROWS, WIDE), jnp.bfloat16),
+        in_specs=[
+            anywhere,
+            vmem,
+            anywhere,
+            anywhere,
+            pl.BlockSpec(memory_space=pltpu.SMEM),
+            vmem,
+            vmem,
+            vmem,
+            vmem,
+        ],
+        out_specs=anywhere,
+        scratch_shapes=[pltpu.VMEM(shape, dtype) for shape, dtype in shapes]
+        + [
+            dma((2, CHUNKS)),
+            dma((ROWS,)),
+            dma,
+            dma,
+            dma((CHUNKS * groups,)),
+            dma((CHUNKS,)),
+            dma((CHUNKS * groups,)),
+            dma((CHUNKS, count)),
+            dma((order_count // ROWS,)),
+        ],
+        cost_estimate=pl.CostEstimate(
+            flops=20 * 10**9, bytes_accessed=40 * 10**6, transcendentals=10**6
+        ),
+        compiler_params=pltpu.CompilerParams(
+            collective_id=0, has_side_effects=True, vmem_limit_bytes=VMEM_CAP
+        ),
+    )(
+        grid_field,
+        norm_gain[None, :],
+        jnp.asarray(high),
+        jnp.asarray(low),
+        jnp.asarray(sine),
+        jnp.asarray(cosine),
+        jnp.asarray((weight * weight_scale).astype(np.float32)),
+        jnp.asarray(logsine),
+        jnp.asarray(log_starts(order_count)),
+    )
+
+
+def filter_kernel(coef_ref, weight_ref, out_ref, full_ref):
+    chunks = coef_ref.shape[0]
+    orders = chunks * ROWS
+    first = pl.program_id(0) * 2 + lax.axis_index("lat") * DEG_DEV
+    both = coef_ref[...].astype(jnp.float32).reshape(chunks, 2, ROWS, WIDE)
+    lines = lax.broadcasted_iota(jnp.int32, (orders, 1), 0)
+
+    @pl.when(pl.program_id(0) == 0)
+    def _():
+        full_ref[...] = jnp.zeros_like(full_ref)
+
+    for odd in range(2):
+        value = both[:, odd].reshape(orders, WIDE)
+        value = jnp.where(lines <= first + odd, value, 0.0).astype(jnp.bfloat16)
+        real, imag = weight_ref[odd, 0], weight_ref[odd, 1]
+        for sample in range(S):
+            for side, halves in enumerate(((real, imag), (-imag, real))):
+                for target, block in enumerate(halves):
+                    row = side * S * C + sample * C
+                    lane = target * S * C + sample * C
+                    full_ref[odd, row : row + C, lane : lane + C] = block
+        out_ref[odd] = jnp.dot(
+            value, full_ref[odd], preferred_element_type=jnp.float32
+        ).astype(out_ref.dtype)
+
+
+def apply_filter(coefficients, filter_weight):
+    chunks = coefficients.shape[0]
+    degrees = filter_weight.shape[0]
+    return pl.pallas_call(
+        filter_kernel,
+        grid=(degrees // 2,),
+        out_shape=jax.ShapeDtypeStruct((degrees, chunks * ROWS, WIDE), jnp.bfloat16),
+        in_specs=[
+            pl.BlockSpec((chunks, 2 * ROWS, WIDE), lambda i: (0, i, 0)),
+            pl.BlockSpec((2, 2, C, C), lambda i: (i, 0, 0, 0)),
+        ],
+        out_specs=pl.BlockSpec((2, chunks * ROWS, WIDE), lambda i: (i, 0, 0)),
+        scratch_shapes=[pltpu.VMEM((2, WIDE, WIDE), jnp.bfloat16)],
+        compiler_params=pltpu.CompilerParams(vmem_limit_bytes=24 * 1024 * 1024),
+    )(coefficients, filter_weight)
+
+
+def body(grid_field, norm_gain, filter_weight):
+    count = lax.axis_size("lat")
+    band, longitudes, columns = grid_field.shape
+    fits = scratch_bytes(scratch_of(count, band, longitudes)) < VMEM_CAP - 6 * 1024 * 1024
+    if count % PLANE or not fits:
+        return plain_body(grid_field, norm_gain, filter_weight)
+    coefficients = coefficients_of(grid_field, norm_gain, count)
+    return apply_filter(coefficients, filter_weight)
+
+
 def solution(mesh):
     in_specs = (P("lat", None, "parts"), P("parts"), P("lat", None, None, "parts"))
     out_specs = P("lat", None, "parts")

time: 260 us -> 179 us (0.69)
  Pallas kernels: 24.3 us -> 175 us
  waiting for transfers between devices: 77.1 us -> 0 us
  local copies, waits for them, and re-layouts: 49.1 us -> 3.58 us
  matrix products: 42 us -> 0 us
  blocking collectives: 25.6 us -> 0 us
  starting transfers between devices: 23.9 us -> 0 us
  other arithmetic: 13.6 us -> 0 us
    pallas_call x2, Pallas kernels: 24.3 us -> 175 us  [the longest x1 168 us: coefficients_of(): pl.pallas_call(functools.partial(spectral_kernel, (count, band, longitude...]
    all_to_all x4 -> x0, waiting for transfers between devices: 77.1 us -> none  [the longest x2 56.2 us: to_degrees(): return lax.all_to_all(sums, 'lat', split_axis=0, concat_axis=0)]
    dot_general x7 -> x0, matrix products: 42 us -> none  [the longest x2 31.1 us: transform(): jnp.einsum('mn,jnx->mjx', jnp.asarray(table), grid_field, precision=lax.P...]
    all_gather x1 -> x0, blocking collectives: 25.6 us -> none  [body(): lax.all_gather(moments, 'lat')]
    all_to_all x4 -> x0, starting transfers between devices: 23.9 us -> none  [the longest x2 12.2 us: to_orders(): lax.all_to_all(raw.astype(jnp.bfloat16), 'lat', split_axis=0, concat_axis...]
    mul x5 -> x0, local copies, waits for them, and re-layouts: 16.6 us -> none  [the longest x4 16.6 us: expand_filter(): mixing.transpose(0, 1, 3, 2, 4)[:, :, None, :, :, None, :]]
    all_to_all x4 -> x0, local copies, waits for them, and re-layouts: 13.7 us -> none  [to_orders(): lax.all_to_all(raw.astype(jnp.bfloat16), 'lat', split_axis=0, concat_axis...]
    reduce_sum x5 -> x0, other arithmetic: 9.04 us -> none  [the longest x1 7.5 us: body(): jnp.einsum('j,jnx->x', sine_own, grid_field * grid_field, precision=lax.P...]
  transfers between devices with their start and end apart: 4 -> 0, of which waited for: 3 -> 0; matrix products, arithmetic and copies ran while one was open for 27% -> 0% of each run, Pallas kernels for 6% -> 0%
where the time goes in v1:
time: 179 us
  Pallas kernels  175 us (98%)
  local copies, waits for them, and re-layouts  3.58 us (2%)
    pallas_call x1, Pallas kernels, coefficients_of(): pl.pallas_call(functools.partial(spectral_kernel, (count, band, longitude...  168 us
    pallas_call x1, Pallas kernels, apply_filter(): pl.pallas_call(filter_kernel, grid=(degrees // 2,), out_shape=jax.ShapeDt...  6.91 us

profile of v1, /device:TPU:29, one launch (start us, length us, event | category | flops | bytes accessed | tf_op | source)
XLA Modules:
  0.0 178.9 jit_solution(9049729682689535344)
XLA Ops:
  0.0 1.5 jit_solution_.3.start_ref
  1.5 0.0 copy-start.1
  1.5 168.3 %shard_map.100.coef_ref = bf16[44,176,256]{2,1,0:T(8,128)(2,1)} custom-call(f32[23,1440,128]{2,1,0:T(8,128)} %field_ref.1, f32[1,64]{1,0:T(1,128)} %bitcast.1, bf16[3,256,1440]{2,1,0:T(8,128)(2,1)} %constant.14.clone.high_ref, bf16[3,256,1440]{2,1,0:T(8,128)(2,1)} %constant.15.clone.low_ref, f32[384]{0:T(512)} %constant.16.clone.sine_ref, ...), custom_call_target="tpu_custom_call" | custom-call | flops 20000000000 | bytes 40000000 | tf_op jit(solution)/shard_map/pallas_call | solution.py:791
  169.8 0.0 copy-done.1
  169.8 0.0 copy-start
  169.8 2.1 %copy-done = bf16[44,176,256]{2,1,0:T(8,128)(2,1)S(1)} copy-done((bf16[44,176,256]{2,1,0:T(8,128)(2,1)S(1)}, bf16[44,176,256]{2,1,0:T(8,128)(2,1)}, u32[]{:S(2)}) %copy-start) | copy-done | bytes 3964952
  172.0 6.9 %shard_map.101 = bf16[22,352,256]{2,1,0:T(8,128)(2,1)} custom-call(bf16[44,176,256]{2,1,0:T(8,128)(2,1)S(1)} %copy-done, bf16[22,2,64,64]{3,2,1,0:T(8,128)(2,1)S(1)} %copy-done.1), custom_call_target="tpu_custom_call" | custom-call | tf_op jit(solution)/shard_map/pallas_call | solution.py:866
Async XLA Ops:
  1.5 168.4 %copy-start.1 = (bf16[22,2,64,64]{3,2,1,0:T(8,128)(2,1)S(1)}, bf16[22,2,64,64]{3,2,1,0:T(8,128)(2,1)}, u32[]{:S(2)}) copy-start(bf16[22,2,64,64]{3,2,1,0:T(8,128)(2,1)} %weight_ref.2) | copy-start | bytes 1081348
  169.8 2.1 %copy-start = (bf16[44,176,256]{2,1,0:T(8,128)(2,1)S(1)}, bf16[44,176,256]{2,1,0:T(8,128)(2,1)}, u32[]{:S(2)}) copy-start(bf16[44,176,256]{2,1,0:T(8,128)(2,1)} %shard_map.100.coef_ref) | copy-start | bytes 11894788

commit v2 on v1

--- a/solution.py
+++ b/solution.py
@@ -259,24 +259,22 @@
 VMEM_CAP = 60 * 1024 * 1024
 
 
-def owner_rank(device):
-    plane, inner = device // PLANE, device % PLANE
-    flip = (inner // 2 + plane) % 2
-    core = inner % 2
-    return flip * (1 + core) + (1 - flip) * (PLANE - 1) * core
+def owns_last(device):
+    return device % PLANE != 1
 
 
 def owner_chunk(device, slot, count):
-    plane = device // PLANE
-    base = PLANE_CHUNKS * (count // PLANE - 1 - plane)
-    return base + PLANE_CHUNKS - 1 - PLANE * slot - owner_rank(device)
+    plane, inner = count // PLANE - 1 - device // PLANE, device % PLANE
+    first = 1 // (plane + inner + 1)
+    at = slot + first * (CHUNKS - 1 - 2 * slot)
+    return PLANE_CHUNKS * plane + PLANE * at + inner - (at // (CHUNKS - 1)) * ((inner + 2) // PLANE)
 
 
 def transform_tables(count, longitudes):
     table = np.zeros((CHUNKS, 2, count, ROWS, longitudes), np.float64)
     for slot in range(CHUNKS):
         for device in range(count):
-            if slot == CHUNKS - 1 and owner_rank(device) == PLANE - 1:
+            if slot == CHUNKS - 1 and not owns_last(device):
                 continue
             orders = owner_chunk(device, slot, count) * ROWS + np.arange(ROWS)
             phases = (orders[:, None] * np.arange(longitudes)[None, :]) % longitudes
@@ -318,7 +316,7 @@
         + 0.5 * (math.lgamma(m + 0.5) - math.lgamma(m + 1.0) - 0.5 * math.log(math.pi))
         for m in range(order_count)
     ]
-    return np.broadcast_to(np.asarray(values, np.float32)[:, None], (order_count, LANES))
+    return np.asarray(values, np.float32)[:, None]
 
 
 def spectral_kernel(
@@ -353,6 +351,7 @@
     lines,
     sums,
     sums_out,
+    blank,
     table_sem,
     stage_sem,
     moment_send,
@@ -362,6 +361,7 @@
     local_sem,
     send_two,
     recv_two,
+    blank_sem,
 ):
     count, band, longitudes, total_sine = sizes
     me = lax.axis_index("lat")
@@ -375,13 +375,11 @@
     kept = table.shape[2]
     width = cosine_ref.shape[1]
     block_rows = DEG_DEV * ROWS
-    zero_owner = [
-        d for d in range(count) if owner_chunk(d, CHUNKS - 1, count) == 0 and owner_rank(d) < PLANE - 1
-    ][0]
-    has_last = owner_rank(me) < PLANE - 1
+    zero_owner = count - PLANE
+    has_last = owns_last(me)
 
     def has_chunk(slot, device):
-        return (slot < CHUNKS - 1) | (owner_rank(device) < PLANE - 1)
+        return (slot < CHUNKS - 1) | owns_last(device)
 
     def table_copies(slot):
         return (
@@ -456,6 +454,12 @@
     take_group(0)
     pl.semaphore_wait(barrier, count - 1)
 
+    def blank_copy(chunk, lines_off):
+        rows = pl.ds(0, lines_off * ROWS)
+        return pltpu.make_async_copy(
+            blank.at[rows], out_ref.at[chunk, rows], blank_sem.at[chunk]
+        )
+
     def moment_copy(device):
         return pltpu.make_async_remote_copy(
             moments,
@@ -485,8 +489,7 @@
             outgoing.at[step, rows], landed.at[slot, slot_of_me, group], local_sem.at[step]
         )
 
-    @pl.loop(0, CHUNKS * groups)
-    def _(step):
+    def transform(step):
         slot, group = step // groups, step % groups
 
         @pl.when((step > 0) & (slot == 0))
@@ -505,22 +508,6 @@
         def _():
             for copy in table_copies(slot):
                 copy.wait()
-
-        @pl.when(step == (CHUNKS - 1) * groups)
-        def _():
-            pltpu.make_async_copy(
-                moments_all.at[pl.ds(0, count - 1)],
-                moments_all.at[pl.ds(0, count - 1)],
-                moment_recv,
-            ).wait()
-            gathered = jnp.sum(moments_all[...], axis=0)
-            first = jnp.sum(gathered[:ROWS], axis=0, keepdims=True) / (longitudes * total_sine)
-            second = jnp.sum(gathered[ROWS:], axis=0, keepdims=True) / (longitudes * total_sine)
-            spread = jnp.sqrt(second - first * first + 1e-05)
-            gain = gain_ref[...]
-            factor = jnp.concatenate([gain] * S, axis=1) / spread
-            scales[:1] = jnp.concatenate([factor, factor], axis=1)
-            scales[1:2] = jnp.concatenate([longitudes * first, jnp.zeros_like(first)], axis=1)
 
         @pl.loop(0, ROWS // 2)
         def _(pair):
@@ -556,8 +543,39 @@
             def _():
                 own_copy(slot, group).start()
 
+    pl.loop(0, (CHUNKS - 1) * groups)(transform)
+
+    pltpu.make_async_copy(
+        moments_all.at[pl.ds(0, count - 1)],
+        moments_all.at[pl.ds(0, count - 1)],
+        moment_recv,
+    ).wait()
+    gathered = jnp.sum(moments_all[...], axis=0)
+    first = jnp.sum(gathered[:ROWS], axis=0, keepdims=True) / (longitudes * total_sine)
+    second = jnp.sum(gathered[ROWS:], axis=0, keepdims=True) / (longitudes * total_sine)
+    spread = jnp.sqrt(second - first * first + 1e-05)
+    gain = gain_ref[...]
+    factor = jnp.concatenate([gain] * S, axis=1) / spread
+    scales[:1] = jnp.concatenate([factor, factor], axis=1)
+    scales[1:2] = jnp.concatenate([longitudes * first, jnp.zeros_like(first)], axis=1)
+
+    blank[...] = jnp.zeros_like(blank)
+
+    @pl.loop(0, out_ref.shape[0])
+    def _(chunk):
+        low_line = chunk * ROWS - me * DEG_DEV
+
+        @pl.when(low_line >= DEG_DEV)
+        def _():
+            pltpu.make_async_copy(blank, out_ref.at[chunk], recv_two.at[chunk]).start()
+
+        for lines_off in range(2, DEG_DEV, 2):
+
+            @pl.when(low_line == lines_off)
+            def _():
+                blank_copy(chunk, lines_off).start()
+
     chunk_of = [owner_chunk(me, slot, count) for slot in range(CHUNKS)]
-    chunk_of[-1] = jnp.maximum(chunk_of[-1], 0)
     lines_in = lax.broadcasted_iota(jnp.int32, (ROWS, width), 0)
     orders = jnp.concatenate(
         [(chunk * ROWS + lines_in).astype(jnp.float32) for chunk in chunk_of], axis=0
@@ -565,11 +583,12 @@
     start = jnp.concatenate(
         [start_ref[pl.ds(pl.multiple_of(chunk * ROWS, ROWS), ROWS), :] for chunk in chunk_of], axis=0
     )
+    start = jnp.broadcast_to(start, (CHUNKS * ROWS, width))
 
     def widen(value):
         return jnp.concatenate([value] * (width // LANES), axis=1)
 
-    log_diag = widen(start) + orders * logsine_ref[...]
+    log_diag = start + orders * logsine_ref[...]
     start_exp = 64.0 * jnp.floor(log_diag / (64.0 * math.log(2.0)))
     exp_ref[...] = start_exp
     mant_ref[...] = jnp.exp(log_diag - start_exp * math.log(2.0))
@@ -621,25 +640,44 @@
                 part_of = lines[lane // LANES, pl.ds(order, BLOCK, stride=order_lines), :]
                 table[order, rows, lane : lane + cut] = part_of[:, :cut].astype(table.dtype)
 
-    def reaches(chunk, device):
-        return chunk * ROWS <= device * DEG_DEV + DEG_DEV - 1
-
-    def degree_copy(slot, device):
+    def rows_from(device, lines_off):
+        base = pl.multiple_of(device * block_rows + lines_off * ROWS, 2 * ROWS)
+        return pl.ds(base, block_rows - lines_off * ROWS)
+
+    def degree_copy(slot, device, lines_off=0):
         chunk = owner_chunk(me, slot, count)
-        rows = pl.ds(pl.multiple_of(device * block_rows, block_rows), block_rows)
         return pltpu.make_async_remote_copy(
-            sums_out.at[slot, rows],
-            out_ref.at[chunk],
+            sums_out.at[slot, rows_from(device, lines_off)],
+            out_ref.at[chunk, rows_from(0, lines_off)],
             send_two.at[slot, device],
             recv_two.at[chunk],
             device_id=(part, device),
             device_id_type=MESH,
         )
 
-    def own_degrees(slot):
+    def own_degrees(slot, lines_off=0):
         chunk = owner_chunk(me, slot, count)
-        rows = pl.ds(pl.multiple_of(me * block_rows, block_rows), block_rows)
-        return pltpu.make_async_copy(sums_out.at[slot, rows], out_ref.at[chunk], recv_two.at[chunk])
+        return pltpu.make_async_copy(
+            sums_out.at[slot, rows_from(me, lines_off)],
+            out_ref.at[chunk, rows_from(0, lines_off)],
+            recv_two.at[chunk],
+        )
+
+    def diagonal(slot, remote, local):
+        first_line = owner_chunk(me, slot, count) * ROWS
+        device = first_line // DEG_DEV
+        for lines_off in range(2, DEG_DEV, 2):
+            hit = first_line - device * DEG_DEV == lines_off
+
+            @pl.when(hit & (device != me))
+            def _():
+                remote(slot, device, lines_off)
+
+            if local is not None:
+
+                @pl.when(hit & (device == me))
+                def _():
+                    local(slot, lines_off)
 
     degree_line = lax.broadcasted_iota(jnp.int32, (degrees, 1), 0)
     sign_even = jnp.where(degree_line % 2 == 0, 1.0, -1.0).astype(jnp.float32)
@@ -677,7 +715,7 @@
             sums_out[slot, rows, :] = jnp.concatenate(
                 [sums[0, rows, :], sums[1, rows, :]], axis=1
             ).astype(jnp.bfloat16)
-            wanted = reaches(owner_chunk(me, slot, count), device)
+            wanted = owner_chunk(me, slot, count) * ROWS <= device * DEG_DEV
 
             @pl.when(wanted & (device != me))
             def _():
@@ -687,11 +725,21 @@
             def _():
                 own_degrees(slot).start()
 
+        diagonal(
+            slot,
+            lambda *where: degree_copy(*where).start(),
+            lambda *where: own_degrees(*where).start(),
+        )
+
     @pl.loop(0, CHUNKS)
     def _(slot):
         @pl.when((slot < CHUNKS - 1) | has_last)
         def _():
             analyse(slot)
+
+        @pl.when(slot == 0)
+        def _():
+            pl.loop((CHUNKS - 1) * groups, CHUNKS * groups)(transform)
 
     pltpu.make_async_copy(
         moments_all.at[pl.ds(0, count - 1)], moments_all.at[pl.ds(0, count - 1)], moment_send
@@ -721,17 +769,35 @@
 
     @pl.loop(0, CHUNKS)
     def _(slot):
-        @pl.loop(0, count)
-        def _(device):
-            wanted = reaches(owner_chunk(me, slot, count), device)
-
-            @pl.when(wanted & (device != me) & has_chunk(slot, me))
+        @pl.when(has_chunk(slot, me))
+        def _():
+            @pl.loop(0, count)
+            def _(device):
+                wanted = owner_chunk(me, slot, count) * ROWS <= device * DEG_DEV
+
+                @pl.when(wanted & (device != me))
+                def _():
+                    degree_copy(slot, device).wait_send()
+
+            diagonal(slot, lambda *where: degree_copy(*where).wait_send(), None)
+
+    @pl.loop(0, out_ref.shape[0])
+    def _(chunk):
+        low_line = chunk * ROWS - me * DEG_DEV
+
+        @pl.when((low_line <= 0) | (low_line >= DEG_DEV))
+        def _():
+            pltpu.make_async_copy(blank, out_ref.at[chunk], recv_two.at[chunk]).wait()
+
+        for lines_off in range(2, DEG_DEV, 2):
+
+            @pl.when(low_line == lines_off)
             def _():
-                degree_copy(slot, device).wait_send()
-
-    @pl.loop(0, (me * DEG_DEV + DEG_DEV - 1) // ROWS + 1)
-    def _(chunk):
-        pltpu.make_async_copy(out_ref.at[chunk], out_ref.at[chunk], recv_two.at[chunk]).wait()
+                blank_copy(chunk, lines_off).wait()
+                rows = rows_from(0, lines_off)
+                pltpu.make_async_copy(
+                    blank.at[rows], out_ref.at[chunk, rows], recv_two.at[chunk]
+                ).wait()
 
 
 def scratch_of(count, band, longitudes):
@@ -765,6 +831,7 @@
         ((width // LANES, BLOCK * order_lines, LANES), f32),
         ((2, degrees * ROWS, LANES), f32),
         ((CHUNKS, degrees * ROWS, WIDE), bf16),
+        ((DEG_DEV * ROWS, WIDE), bf16),
     ]
 
 
@@ -814,6 +881,7 @@
             dma((CHUNKS * groups,)),
             dma((CHUNKS, count)),
             dma((order_count // ROWS,)),
+            dma((order_count // ROWS,)),
         ],
         cost_estimate=pl.CostEstimate(
             flops=20 * 10**9, bytes_accessed=40 * 10**6, transcendentals=10**6
@@ -834,46 +902,67 @@
     )
 
 
-def filter_kernel(coef_ref, weight_ref, out_ref, full_ref):
-    chunks = coef_ref.shape[0]
+def filter_kernel(coef_ref, weight_ref, out_ref, coefs, outs, full_ref, in_sem, out_sem):
+    pairs = coefs.shape[0]
+    chunks = coefs.shape[1]
     orders = chunks * ROWS
-    first = pl.program_id(0) * 2 + lax.axis_index("lat") * DEG_DEV
-    both = coef_ref[...].astype(jnp.float32).reshape(chunks, 2, ROWS, WIDE)
-    lines = lax.broadcasted_iota(jnp.int32, (orders, 1), 0)
-
-    @pl.when(pl.program_id(0) == 0)
-    def _():
-        full_ref[...] = jnp.zeros_like(full_ref)
-
-    for odd in range(2):
-        value = both[:, odd].reshape(orders, WIDE)
-        value = jnp.where(lines <= first + odd, value, 0.0).astype(jnp.bfloat16)
-        real, imag = weight_ref[odd, 0], weight_ref[odd, 1]
-        for sample in range(S):
-            for side, halves in enumerate(((real, imag), (-imag, real))):
-                for target, block in enumerate(halves):
-                    row = side * S * C + sample * C
-                    lane = target * S * C + sample * C
-                    full_ref[odd, row : row + C, lane : lane + C] = block
-        out_ref[odd] = jnp.dot(
-            value, full_ref[odd], preferred_element_type=jnp.float32
-        ).astype(out_ref.dtype)
+
+    def fetch(pair):
+        rows = pl.ds(pl.multiple_of(pair * 2 * ROWS, 2 * ROWS), 2 * ROWS)
+        return pltpu.make_async_copy(coef_ref.at[:, rows, :], coefs.at[pair], in_sem.at[pair])
+
+    def store(pair):
+        return pltpu.make_async_copy(
+            outs.at[pair], out_ref.at[pl.ds(2 * pair, 2)], out_sem.at[pair]
+        )
+
+    for pair in range(pairs):
+        fetch(pair).start()
+    full_ref[...] = jnp.zeros_like(full_ref)
+
+    @pl.loop(0, pairs)
+    def _(pair):
+        for odd in range(2):
+            real, imag = weight_ref[2 * pair + odd, 0], weight_ref[2 * pair + odd, 1]
+            for sample in range(S):
+                for side, halves in enumerate(((real, imag), (-imag, real))):
+                    for target, block in enumerate(halves):
+                        row = side * S * C + sample * C
+                        lane = target * S * C + sample * C
+                        full_ref[odd, row : row + C, lane : lane + C] = block
+        fetch(pair).wait()
+        both = coefs[pair].astype(jnp.float32).reshape(chunks, 2, ROWS, WIDE)
+        for odd in range(2):
+            value = both[:, odd].reshape(orders, WIDE).astype(jnp.bfloat16)
+            outs[pair, odd] = jnp.dot(
+                value, full_ref[odd], preferred_element_type=jnp.float32
+            ).astype(outs.dtype)
+        store(pair).start()
+
+    @pl.loop(0, pairs)
+    def _(pair):
+        store(pair).wait()
 
 
 def apply_filter(coefficients, filter_weight):
     chunks = coefficients.shape[0]
     degrees = filter_weight.shape[0]
+    pairs = degrees // 2
+    orders = chunks * ROWS
+    anywhere = pl.BlockSpec(memory_space=pl.ANY)
     return pl.pallas_call(
         filter_kernel,
-        grid=(degrees // 2,),
-        out_shape=jax.ShapeDtypeStruct((degrees, chunks * ROWS, WIDE), jnp.bfloat16),
-        in_specs=[
-            pl.BlockSpec((chunks, 2 * ROWS, WIDE), lambda i: (0, i, 0)),
-            pl.BlockSpec((2, 2, C, C), lambda i: (i, 0, 0, 0)),
+        out_shape=jax.ShapeDtypeStruct((degrees, orders, WIDE), jnp.bfloat16),
+        in_specs=[anywhere, pl.BlockSpec(memory_space=pltpu.VMEM)],
+        out_specs=anywhere,
+        scratch_shapes=[
+            pltpu.VMEM((pairs, chunks, 2 * ROWS, WIDE), jnp.bfloat16),
+            pltpu.VMEM((pairs, 2, orders, WIDE), jnp.bfloat16),
+            pltpu.VMEM((2, WIDE, WIDE), jnp.bfloat16),
+            pltpu.SemaphoreType.DMA((pairs,)),
+            pltpu.SemaphoreType.DMA((pairs,)),
         ],
-        out_specs=pl.BlockSpec((2, chunks * ROWS, WIDE), lambda i: (i, 0, 0)),
-        scratch_shapes=[pltpu.VMEM((2, WIDE, WIDE), jnp.bfloat16)],
-        compiler_params=pltpu.CompilerParams(vmem_limit_bytes=24 * 1024 * 1024),
+        compiler_params=pltpu.CompilerParams(vmem_limit_bytes=VMEM_CAP),
     )(coefficients, filter_weight)
 
 

time: 179 us -> 168 us (0.939)
  Pallas kernels: 175 us -> 166 us
  local copies, waits for them, and re-layouts: 3.58 us -> 0 us
    pallas_call x1, Pallas kernels: 168 us -> 159 us  [coefficients_of(): pl.pallas_call(functools.partial(spectral_kernel, (count, band, longitude...]
    unnamed x4 -> x0, local copies, waits for them, and re-layouts: 2.12 us -> none
where the time goes in v2:
time: 168 us; the launch traced here: 166 us
  Pallas kernels  166 us (99%)
    pallas_call x1, Pallas kernels, coefficients_of(): pl.pallas_call(functools.partial(spectral_kernel, (count, band, longitude...  159 us
    pallas_call x1, Pallas kernels, apply_filter(): pl.pallas_call(filter_kernel, out_shape=jax.ShapeDtypeStruct((degrees, or...  6.99 us

profile of v2, /device:TPU:29, one launch (start us, length us, event | category | flops | bytes accessed | tf_op | source)
XLA Modules:
  0.0 166.3 jit_solution(10962522652360927777)
XLA Ops:
  0.0 159.3 %shard_map.100.coef_ref = bf16[44,176,256]{2,1,0:T(8,128)(2,1)} custom-call(f32[23,1440,128]{2,1,0:T(8,128)} %field_ref.1, f32[1,64]{1,0:T(1,128)} %bitcast.1, bf16[3,256,1440]{2,1,0:T(8,128)(2,1)} %constant.14.clone.high_ref, bf16[3,256,1440]{2,1,0:T(8,128)(2,1)} %constant.15.clone.low_ref, f32[384]{0:T(512)} %constant.16.clone.sine_ref, ...), custom_call_target="tpu_custom_call" | custom-call | flops 20000000000 | bytes 40000000 | tf_op jit(solution)/shard_map/pallas_call | solution.py:858
  159.3 7.0 %shard_map.101 = bf16[22,352,256]{2,1,0:T(8,128)(2,1)} custom-call(bf16[44,176,256]{2,1,0:T(8,128)(2,1)} %shard_map.100.coef_ref, bf16[22,2,64,64]{3,2,1,0:T(8,128)(2,1)} %weight_ref.2), custom_call_target="tpu_custom_call" | custom-call | tf_op jit(solution)/shard_map/pallas_call | solution.py:953

commit v3 on v2

--- a/solution.py
+++ b/solution.py
@@ -663,21 +663,45 @@
             recv_two.at[chunk],
         )
 
-    def diagonal(slot, remote, local):
+    upper = count - count // PLANE
+
+    def crosses(device):
+        return (device >= upper) != (me >= upper)
+
+    def each_target(slot, chosen, remote, local):
         first_line = owner_chunk(me, slot, count) * ROWS
+
+        @pl.loop(1, count)
+        def _(ahead):
+            device = (me + ahead) % count
+
+            @pl.when((first_line <= device * DEG_DEV) & chosen(device))
+            def _():
+                remote(slot, device, 0)
+
+        @pl.when((first_line <= me * DEG_DEV) & chosen(me))
+        def _():
+            local(slot, 0)
+
         device = first_line // DEG_DEV
         for lines_off in range(2, DEG_DEV, 2):
-            hit = first_line - device * DEG_DEV == lines_off
+            hit = (first_line - device * DEG_DEV == lines_off) & chosen(device)
 
             @pl.when(hit & (device != me))
             def _():
                 remote(slot, device, lines_off)
 
-            if local is not None:
-
-                @pl.when(hit & (device == me))
-                def _():
-                    local(slot, lines_off)
+            @pl.when(hit & (device == me))
+            def _():
+                local(slot, lines_off)
+
+    def send_degrees(slot, chosen):
+        each_target(
+            slot,
+            chosen,
+            lambda *where: degree_copy(*where).start(),
+            lambda *where: own_degrees(*where).start(),
+        )
 
     degree_line = lax.broadcasted_iota(jnp.int32, (degrees, 1), 0)
     sign_even = jnp.where(degree_line % 2 == 0, 1.0, -1.0).astype(jnp.float32)
@@ -709,37 +733,26 @@
                     ]
 
         @pl.loop(0, count)
-        def _(ahead):
-            device = (me + 1 + ahead) % count
+        def _(device):
             rows = pl.ds(pl.multiple_of(device * block_rows, block_rows), block_rows)
             sums_out[slot, rows, :] = jnp.concatenate(
                 [sums[0, rows, :], sums[1, rows, :]], axis=1
             ).astype(jnp.bfloat16)
-            wanted = owner_chunk(me, slot, count) * ROWS <= device * DEG_DEV
-
-            @pl.when(wanted & (device != me))
-            def _():
-                degree_copy(slot, device).start()
-
-            @pl.when(wanted & (device == me))
-            def _():
-                own_degrees(slot).start()
-
-        diagonal(
-            slot,
-            lambda *where: degree_copy(*where).start(),
-            lambda *where: own_degrees(*where).start(),
-        )
 
     @pl.loop(0, CHUNKS)
     def _(slot):
         @pl.when((slot < CHUNKS - 1) | has_last)
         def _():
             analyse(slot)
+            send_degrees(slot, crosses)
 
         @pl.when(slot == 0)
         def _():
             pl.loop((CHUNKS - 1) * groups, CHUNKS * groups)(transform)
+
+        @pl.when((slot < CHUNKS - 1) | has_last)
+        def _():
+            send_degrees(slot, lambda device: jnp.logical_not(crosses(device)))
 
     pltpu.make_async_copy(
         moments_all.at[pl.ds(0, count - 1)], moments_all.at[pl.ds(0, count - 1)], moment_send
@@ -771,15 +784,12 @@
     def _(slot):
         @pl.when(has_chunk(slot, me))
         def _():
-            @pl.loop(0, count)
-            def _(device):
-                wanted = owner_chunk(me, slot, count) * ROWS <= device * DEG_DEV
-
-                @pl.when(wanted & (device != me))
-                def _():
-                    degree_copy(slot, device).wait_send()
-
-            diagonal(slot, lambda *where: degree_copy(*where).wait_send(), None)
+            each_target(
+                slot,
+                lambda device: device >= 0,
+                lambda *where: degree_copy(*where).wait_send(),
+                lambda *where: None,
+            )
 
     @pl.loop(0, out_ref.shape[0])
     def _(chunk):

time: 168 us -> 161 us (0.958)
  Pallas kernels: 166 us -> 160 us
    pallas_call x1, Pallas kernels: 159 us -> 153 us  [coefficients_of(): pl.pallas_call(functools.partial(spectral_kernel, (count, band, longitude...]
where the time goes in v3:
time: 161 us; the launch traced here: 160 us
  Pallas kernels  160 us (99%)
    pallas_call x1, Pallas kernels, coefficients_of(): pl.pallas_call(functools.partial(spectral_kernel, (count, band, longitude...  153 us
    pallas_call x1, Pallas kernels, apply_filter(): pl.pallas_call(filter_kernel, out_shape=jax.ShapeDtypeStruct((degrees, or...  6.99 us

profile of v3, /device:TPU:29, one launch (start us, length us, event | category | flops | bytes accessed | tf_op | source)
XLA Modules:
  0.0 160.1 jit_solution(6113618155801768056)
XLA Ops:
  0.0 153.1 %shard_map.100.coef_ref = bf16[44,176,256]{2,1,0:T(8,128)(2,1)} custom-call(f32[23,1440,128]{2,1,0:T(8,128)} %field_ref.1, f32[1,64]{1,0:T(1,128)} %bitcast.1, bf16[3,256,1440]{2,1,0:T(8,128)(2,1)} %constant.14.clone.high_ref, bf16[3,256,1440]{2,1,0:T(8,128)(2,1)} %constant.15.clone.low_ref, f32[384]{0:T(512)} %constant.16.clone.sine_ref, ...), custom_call_target="tpu_custom_call" | custom-call | flops 20000000000 | bytes 40000000 | tf_op jit(solution)/shard_map/pallas_call | solution.py:868
  153.1 7.0 %shard_map.101 = bf16[22,352,256]{2,1,0:T(8,128)(2,1)} custom-call(bf16[44,176,256]{2,1,0:T(8,128)(2,1)} %shard_map.100.coef_ref, bf16[22,2,64,64]{3,2,1,0:T(8,128)(2,1)} %weight_ref.2), custom_call_target="tpu_custom_call" | custom-call | tf_op jit(solution)/shard_map/pallas_call | solution.py:963

commit v4 on v3

--- a/solution.py
+++ b/solution.py
@@ -352,6 +352,11 @@
     sums,
     sums_out,
     blank,
+    held,
+    paired,
+    landed_pair,
+    spread_out,
+    pair_sems,
     table_sem,
     stage_sem,
     moment_send,
@@ -418,8 +423,7 @@
 
     piece = longitudes // 6
 
-    def take_row(place, lanes):
-        row_copy(place).wait()
+    def split_row(place, lanes):
         at = place % ROWS
         pair = place // 2
         total = jnp.zeros((ROWS, LANES), jnp.float32)
@@ -437,6 +441,10 @@
         moments[:ROWS] += sine * total
         moments[ROWS:] += sine * square
 
+    def take_row(place, lanes):
+        row_copy(place).wait()
+        split_row(place, lanes)
+
         @pl.when(place + ROWS < band)
         def _():
             row_copy(place + ROWS).start()
@@ -451,7 +459,37 @@
             def _():
                 take_row(place + 1, slice(LANES, WIDE))
 
-    take_group(0)
+    halves = (slice(0, LANES), slice(LANES, WIDE))
+    lines_of = count * ROWS
+
+    def project(slot, at):
+        product = jnp.dot(high[slot], field_high[at], preferred_element_type=jnp.float32)
+        product += jnp.dot(high[slot], field_low[at], preferred_element_type=jnp.float32)
+        product += jnp.dot(low[slot], field_high[at], preferred_element_type=jnp.float32)
+        return product
+
+    def turn(product, pair):
+        for side in range(2):
+            for row in range(2):
+                turned[side, pl.ds(2 * pair + row, lines_of, stride=ROWS), :] = product[
+                    side * lines_of : (side + 1) * lines_of, row * LANES : (row + 1) * LANES
+                ]
+
+    for row in range(2):
+        take_row(row, halves[row])
+    for copy in table_copies(0):
+        copy.wait()
+    for pair in range(ROWS // 2):
+        following = range(2 * pair + 2, 2 * pair + 4) if pair + 1 < ROWS // 2 else ()
+        for place in following:
+            row_copy(place).wait()
+        product = project(0, pair)
+        for place in following:
+            split_row(place, halves[place % 2])
+        turn(product, pair)
+        for place in following:
+            if place + ROWS < band:
+                row_copy(place + ROWS).start()
     pl.semaphore_wait(barrier, count - 1)
 
     def blank_copy(chunk, lines_off):
@@ -489,75 +527,121 @@
             outgoing.at[step, rows], landed.at[slot, slot_of_me, group], local_sem.at[step]
         )
 
+    short = ROWS * (ROWS - 1)
+
+    def pair_copy(device):
+        return pltpu.make_async_remote_copy(
+            paired.at[device],
+            landed_pair.at[slot_of_me],
+            pair_sems.at[0],
+            pair_sems.at[1],
+            device_id=(part, device),
+            device_id_type=MESH,
+        )
+
+    def own_pair():
+        return pltpu.make_async_copy(
+            paired.at[me], landed_pair.at[slot_of_me], pair_sems.at[2]
+        )
+
+    def fold_last():
+        @pl.loop(0, count)
+        def _(device):
+            first = device * ROWS * ROWS
+            for side in range(2):
+                last = turned[side, pl.ds(pl.multiple_of(first + short, ROWS), ROWS), :]
+                turned[side, pl.ds(first + ROWS - 1, ROWS, stride=ROWS), :] = last
+
+    def send_pairs():
+        @pl.loop(0, count)
+        def _(ahead):
+            device = (me + 1 + ahead) % count
+            rows = pl.ds(pl.multiple_of(device * ROWS * ROWS, ROWS), short)
+            paired[device] = jnp.concatenate(
+                [
+                    jnp.concatenate([source[0, rows, :], source[1, rows, :]], axis=1)
+                    for source in (held, turned)
+                ],
+                axis=0,
+            ).astype(jnp.bfloat16)
+
+            @pl.when(device != me)
+            def _():
+                pair_copy(device).start()
+
+            @pl.when(device == me)
+            def _():
+                own_pair().start()
+
+    upper = count - count // PLANE
+
+    def crosses(device):
+        return (device >= upper) != (me >= upper)
+
     def transform(step):
         slot, group = step // groups, step % groups
 
-        @pl.when((step > 0) & (slot == 0))
-        def _():
-            take_group(group)
-
-        @pl.when(step == groups - 1)
-        def _():
+        @pl.when(step == 1)
+        def _():
+            pl.loop(1, groups)(take_group)
             moments_all[me] = moments[...]
 
             @pl.loop(1, count)
             def _(ahead):
                 moment_copy((me + ahead) % count).start()
 
-        @pl.when(group == 0)
+        @pl.when((step == 2 * groups - 1) | (step == 2 * groups))
         def _():
             for copy in table_copies(slot):
                 copy.wait()
 
-        @pl.loop(0, ROWS // 2)
-        def _(pair):
-            at = group * (ROWS // 2) + pair
-            product = jnp.dot(high[slot], field_high[at], preferred_element_type=jnp.float32)
-            product += jnp.dot(high[slot], field_low[at], preferred_element_type=jnp.float32)
-            product += jnp.dot(low[slot], field_high[at], preferred_element_type=jnp.float32)
-            lines_of = count * ROWS
-            for side in range(2):
-                for row in range(2):
-                    turned[side, pl.ds(2 * pair + row, lines_of, stride=ROWS), :] = product[
-                        side * lines_of : (side + 1) * lines_of, row * LANES : (row + 1) * LANES
-                    ]
+        @pl.when(step > 0)
+        def _():
+            @pl.loop(0, ROWS // 2)
+            def _(pair):
+                turn(project(slot, group * (ROWS // 2) + pair), pair)
 
         @pl.when(slot == CHUNKS - 1)
         def _():
             at = zero_owner * ROWS * ROWS
             turned[0, at : at + ROWS, :] -= scales[1:2, :LANES]
 
-        @pl.loop(0, count)
-        def _(ahead):
-            device = (me + 1 + ahead) % count
-            rows = pl.ds(pl.multiple_of(device * ROWS * ROWS, ROWS * ROWS), ROWS * ROWS)
-            outgoing[step, rows, :] = jnp.concatenate(
-                [turned[0, rows, :], turned[1, rows, :]], axis=1
-            ).astype(jnp.bfloat16)
-
-            @pl.when((device != me) & has_chunk(slot, device))
+        folded = (group == groups - 1) & (slot < CHUNKS - 1)
+
+        @pl.when(jnp.logical_not(folded))
+        def _():
+            @pl.loop(0, count)
+            def _(ahead):
+                device = (me + 1 + ahead) % count
+                rows = pl.ds(pl.multiple_of(device * ROWS * ROWS, ROWS * ROWS), ROWS * ROWS)
+                outgoing[step, rows, :] = jnp.concatenate(
+                    [turned[0, rows, :], turned[1, rows, :]], axis=1
+                ).astype(jnp.bfloat16)
+
+                @pl.when((device != me) & has_chunk(slot, device))
+                def _():
+                    order_copy(slot, group, device).start()
+
+                @pl.when((device == me) & has_chunk(slot, device))
+                def _():
+                    own_copy(slot, group).start()
+
+        @pl.when(folded)
+        def _():
+            fold_last()
+
+            @pl.when(slot == 0)
             def _():
-                order_copy(slot, group, device).start()
-
-            @pl.when((device == me) & has_chunk(slot, device))
+                held[...] = turned[...]
+
+            @pl.when(slot > 0)
             def _():
-                own_copy(slot, group).start()
-
-    pl.loop(0, (CHUNKS - 1) * groups)(transform)
-
-    pltpu.make_async_copy(
-        moments_all.at[pl.ds(0, count - 1)],
-        moments_all.at[pl.ds(0, count - 1)],
-        moment_recv,
-    ).wait()
-    gathered = jnp.sum(moments_all[...], axis=0)
-    first = jnp.sum(gathered[:ROWS], axis=0, keepdims=True) / (longitudes * total_sine)
-    second = jnp.sum(gathered[ROWS:], axis=0, keepdims=True) / (longitudes * total_sine)
-    spread = jnp.sqrt(second - first * first + 1e-05)
-    gain = gain_ref[...]
-    factor = jnp.concatenate([gain] * S, axis=1) / spread
-    scales[:1] = jnp.concatenate([factor, factor], axis=1)
-    scales[1:2] = jnp.concatenate([longitudes * first, jnp.zeros_like(first)], axis=1)
+                send_pairs()
+
+    @pl.loop(0, groups + 2)
+    def _(turn_at):
+        tail = groups + (groups - 1) * (groups + 1 - turn_at)
+        transform(jnp.where(turn_at < groups, turn_at, tail))
 
     blank[...] = jnp.zeros_like(blank)
 
@@ -663,11 +747,6 @@
             recv_two.at[chunk],
         )
 
-    upper = count - count // PLANE
-
-    def crosses(device):
-        return (device >= upper) != (me >= upper)
-
     def each_target(slot, chosen, remote, local):
         first_line = owner_chunk(me, slot, count) * ROWS
 
@@ -706,14 +785,47 @@
     degree_line = lax.broadcasted_iota(jnp.int32, (degrees, 1), 0)
     sign_even = jnp.where(degree_line % 2 == 0, 1.0, -1.0).astype(jnp.float32)
 
+    def unfold():
+        blocks = landed_pair.at[pl.ds(0, count - 1)]
+        pltpu.make_async_copy(blocks, blocks, pair_sems.at[1]).wait()
+        own_pair().wait()
+        spread_out[...] = jnp.zeros_like(spread_out)
+
+        @pl.loop(0, count)
+        def _(source):
+            value = landed_pair[source].astype(jnp.float32)
+            for lane in range(2):
+                spread_out[lane, : 2 * short, :] = value[:, lane * LANES : (lane + 1) * LANES]
+            for slot in range(2):
+                last = jnp.concatenate(
+                    [
+                        spread_out[lane, pl.ds(slot * short + ROWS - 1, ROWS, stride=ROWS), :]
+                        for lane in range(2)
+                    ],
+                    axis=1,
+                )
+                landed[slot, source, groups - 1] = jnp.concatenate(
+                    [value[slot * short : (slot + 1) * short], last], axis=0
+                ).astype(landed.dtype)
+
     def analyse(slot):
-        pltpu.make_async_copy(
-            landed.at[slot, pl.ds(0, count - 1)],
-            landed.at[slot, pl.ds(0, count - 1)],
-            recv_sem.at[slot],
-        ).wait()
-        for group in range(groups):
-            own_copy(slot, group).wait()
+        def wait_landed(parts):
+            blocks = landed.at[slot, pl.ds(0, count - 1), pl.ds(0, parts)]
+            pltpu.make_async_copy(blocks, blocks, recv_sem.at[slot]).wait()
+            for group in range(parts):
+                own_copy(slot, group).wait()
+
+        @pl.when(slot < CHUNKS - 1)
+        def _():
+            wait_landed(groups - 1)
+
+        @pl.when(slot == CHUNKS - 1)
+        def _():
+            wait_landed(groups)
+
+        @pl.when(slot == 0)
+        def _():
+            unfold()
 
         @pl.loop(0, ROWS // 2)
         def _(pair):
@@ -739,16 +851,31 @@
                 [sums[0, rows, :], sums[1, rows, :]], axis=1
             ).astype(jnp.bfloat16)
 
+    pltpu.make_async_copy(
+        moments_all.at[pl.ds(0, count - 1)],
+        moments_all.at[pl.ds(0, count - 1)],
+        moment_recv,
+    ).wait()
+    gathered = jnp.sum(moments_all[...], axis=0)
+    first = jnp.sum(gathered[:ROWS], axis=0, keepdims=True) / (longitudes * total_sine)
+    second = jnp.sum(gathered[ROWS:], axis=0, keepdims=True) / (longitudes * total_sine)
+    spread = jnp.sqrt(second - first * first + 1e-05)
+    gain = gain_ref[...]
+    factor = jnp.concatenate([gain] * S, axis=1) / spread
+    scales[:1] = jnp.concatenate([factor, factor], axis=1)
+    scales[1:2] = jnp.concatenate([longitudes * first, jnp.zeros_like(first)], axis=1)
+
+    @pl.loop(0, 2 * groups - 2)
+    def _(turn_at):
+        late = turn_at < groups - 2
+        transform(jnp.where(late, turn_at + groups + 1, turn_at + groups + 2))
+
     @pl.loop(0, CHUNKS)
     def _(slot):
         @pl.when((slot < CHUNKS - 1) | has_last)
         def _():
             analyse(slot)
             send_degrees(slot, crosses)
-
-        @pl.when(slot == 0)
-        def _():
-            pl.loop((CHUNKS - 1) * groups, CHUNKS * groups)(transform)
 
         @pl.when((slot < CHUNKS - 1) | has_last)
         def _():
@@ -764,9 +891,11 @@
             outgoing.at[step, rows], outgoing.at[step, rows], send_sem.at[step]
         ).wait()
 
-    @pl.loop(0, (CHUNKS - 1) * groups)
-    def _(step):
-        wait_orders(step, count - 1)
+    for slot in range(CHUNKS - 1):
+        for group in range(groups - 1):
+            wait_orders(slot * groups + group, count - 1)
+    blocks = paired.at[pl.ds(0, count - 1)]
+    pltpu.make_async_copy(blocks, blocks, pair_sems.at[0]).wait()
 
     last_owners = count - count // PLANE
 
@@ -842,6 +971,10 @@
         ((2, degrees * ROWS, LANES), f32),
         ((CHUNKS, degrees * ROWS, WIDE), bf16),
         ((DEG_DEV * ROWS, WIDE), bf16),
+        ((2, lines_of * ROWS, LANES), f32),
+        ((count, 2 * ROWS * (ROWS - 1), WIDE), bf16),
+        ((count, 2 * ROWS * (ROWS - 1), WIDE), bf16),
+        ((2, 2 * ROWS * ROWS, LANES), f32),
     ]
 
 
@@ -882,6 +1015,7 @@
         out_specs=anywhere,
         scratch_shapes=[pltpu.VMEM(shape, dtype) for shape, dtype in shapes]
         + [
+            dma((3,)),
             dma((2, CHUNKS)),
             dma((ROWS,)),
             dma,
@@ -928,24 +1062,24 @@
 
     for pair in range(pairs):
         fetch(pair).start()
+
     full_ref[...] = jnp.zeros_like(full_ref)
-
-    @pl.loop(0, pairs)
-    def _(pair):
+    for pair in range(pairs):
         for odd in range(2):
-            real, imag = weight_ref[2 * pair + odd, 0], weight_ref[2 * pair + odd, 1]
+            degree = 2 * pair + odd
+            real, imag = weight_ref[degree, 0], weight_ref[degree, 1]
             for sample in range(S):
                 for side, halves in enumerate(((real, imag), (-imag, real))):
                     for target, block in enumerate(halves):
                         row = side * S * C + sample * C
                         lane = target * S * C + sample * C
-                        full_ref[odd, row : row + C, lane : lane + C] = block
+                        full_ref[degree, row : row + C, lane : lane + C] = block
         fetch(pair).wait()
         both = coefs[pair].astype(jnp.float32).reshape(chunks, 2, ROWS, WIDE)
         for odd in range(2):
             value = both[:, odd].reshape(orders, WIDE).astype(jnp.bfloat16)
             outs[pair, odd] = jnp.dot(
-                value, full_ref[odd], preferred_element_type=jnp.float32
+                value, full_ref[2 * pair + odd], preferred_element_type=jnp.float32
             ).astype(outs.dtype)
         store(pair).start()
 
@@ -968,7 +1102,7 @@
         scratch_shapes=[
             pltpu.VMEM((pairs, chunks, 2 * ROWS, WIDE), jnp.bfloat16),
             pltpu.VMEM((pairs, 2, orders, WIDE), jnp.bfloat16),
-            pltpu.VMEM((2, WIDE, WIDE), jnp.bfloat16),
+            pltpu.VMEM((degrees, WIDE, WIDE), jnp.bfloat16),
             pltpu.SemaphoreType.DMA((pairs,)),
             pltpu.SemaphoreType.DMA((pairs,)),
         ],
@@ -979,8 +1113,8 @@
 def body(grid_field, norm_gain, filter_weight):
     count = lax.axis_size("lat")
     band, longitudes, columns = grid_field.shape
-    fits = scratch_bytes(scratch_of(count, band, longitudes)) < VMEM_CAP - 6 * 1024 * 1024
-    if count % PLANE or not fits:
+    fits = scratch_bytes(scratch_of(count, band, longitudes)) < VMEM_CAP - 3 * 1024 * 1024
+    if count % PLANE or band % ROWS != ROWS - 1 or band < 2 * ROWS or not fits:
         return plain_body(grid_field, norm_gain, filter_weight)
     coefficients = coefficients_of(grid_field, norm_gain, count)
     return apply_filter(coefficients, filter_weight)

time: 161 us -> 157 us (0.975)
  Pallas kernels: 160 us -> 155 us
    pallas_call x1, Pallas kernels: 153 us -> 149 us  [coefficients_of(): pl.pallas_call(functools.partial(spectral_kernel, (count, band, longitude...]
where the time goes in v4:
time: 157 us; the launch traced here: 155 us
  Pallas kernels  155 us (99%)
    pallas_call x1, Pallas kernels, coefficients_of(): pl.pallas_call(functools.partial(spectral_kernel, (count, band, longitude...  149 us
    pallas_call x1, Pallas kernels, apply_filter(): pl.pallas_call(filter_kernel, out_shape=jax.ShapeDtypeStruct((degrees, or...  5.92 us

profile of v4, /device:TPU:29, one launch (start us, length us, event | category | flops | bytes accessed | tf_op | source)
XLA Modules:
  0.0 155.3 jit_solution(3889681813277036904)
XLA Ops:
  0.0 149.3 %shard_map.100.coef_ref = bf16[44,176,256]{2,1,0:T(8,128)(2,1)} custom-call(f32[23,1440,128]{2,1,0:T(8,128)} %field_ref.1, f32[1,64]{1,0:T(1,128)} %bitcast.1, bf16[3,256,1440]{2,1,0:T(8,128)(2,1)} %constant.14.clone.high_ref, bf16[3,256,1440]{2,1,0:T(8,128)(2,1)} %constant.15.clone.low_ref, f32[384]{0:T(512)} %constant.16.clone.sine_ref, ...), custom_call_target="tpu_custom_call" | custom-call | flops 20000000000 | bytes 40000000 | tf_op jit(solution)/shard_map/pallas_call | solution.py:1001
  149.4 5.9 %shard_map.101 = bf16[22,352,256]{2,1,0:T(8,128)(2,1)} custom-call(bf16[44,176,256]{2,1,0:T(8,128)(2,1)} %shard_map.100.coef_ref, bf16[22,2,64,64]{3,2,1,0:T(8,128)(2,1)} %weight_ref.2), custom_call_target="tpu_custom_call" | custom-call | tf_op jit(solution)/shard_map/pallas_call | solution.py:1097

commit v5 on v4

--- a/solution.py
+++ b/solution.py
@@ -475,22 +475,6 @@
                     side * lines_of : (side + 1) * lines_of, row * LANES : (row + 1) * LANES
                 ]
 
-    for row in range(2):
-        take_row(row, halves[row])
-    for copy in table_copies(0):
-        copy.wait()
-    for pair in range(ROWS // 2):
-        following = range(2 * pair + 2, 2 * pair + 4) if pair + 1 < ROWS // 2 else ()
-        for place in following:
-            row_copy(place).wait()
-        product = project(0, pair)
-        for place in following:
-            split_row(place, halves[place % 2])
-        turn(product, pair)
-        for place in following:
-            if place + ROWS < band:
-                row_copy(place + ROWS).start()
-    pl.semaphore_wait(barrier, count - 1)
 
     def blank_copy(chunk, lines_off):
         rows = pl.ds(0, lines_off * ROWS)
@@ -555,7 +539,7 @@
     def send_pairs():
         @pl.loop(0, count)
         def _(ahead):
-            device = (me + 1 + ahead) % count
+            device = ((me // half + 1 + ahead // half) % 2) * half + (me + ahead) % half
             rows = pl.ds(pl.multiple_of(device * ROWS * ROWS, ROWS), short)
             paired[device] = jnp.concatenate(
                 [
@@ -578,6 +562,70 @@
     def crosses(device):
         return (device >= upper) != (me >= upper)
 
+    def send_group(slot, group, first, last):
+        @pl.loop(first, last)
+        def _(ahead):
+            device = ((me // half + 1 + ahead // half) % 2) * half + (me + ahead) % half
+            rows = pl.ds(pl.multiple_of(device * ROWS * ROWS, ROWS * ROWS), ROWS * ROWS)
+            outgoing[slot * groups + group, rows, :] = jnp.concatenate(
+                [turned[0, rows, :], turned[1, rows, :]], axis=1
+            ).astype(jnp.bfloat16)
+
+            @pl.when((device != me) & has_chunk(slot, device))
+            def _():
+                order_copy(slot, group, device).start()
+
+            @pl.when((device == me) & has_chunk(slot, device))
+            def _():
+                own_copy(slot, group).start()
+
+    def project_half(pair, part_of):
+        lines_half = half * ROWS
+        rows = [
+            pl.ds(pl.multiple_of(side * lines_of + part_of * lines_half, lines_half), lines_half)
+            for side in range(2)
+        ]
+        top = jnp.concatenate([high[0, row, :] for row in rows], axis=0)
+        rest = jnp.concatenate([low[0, row, :] for row in rows], axis=0)
+        product = jnp.dot(top, field_high[pair], preferred_element_type=jnp.float32)
+        product += jnp.dot(top, field_low[pair], preferred_element_type=jnp.float32)
+        product += jnp.dot(rest, field_high[pair], preferred_element_type=jnp.float32)
+        return product
+
+    def turn_half(product, pair, part_of):
+        lines_half = half * ROWS
+        for side in range(2):
+            for row in range(2):
+                at = part_of * lines_half * ROWS + 2 * pair + row
+                turned[side, pl.ds(at, lines_half, stride=ROWS), :] = product[
+                    side * lines_half : (side + 1) * lines_half, row * LANES : (row + 1) * LANES
+                ]
+
+    for row in range(2):
+        take_row(row, halves[row])
+    for copy in table_copies(0):
+        copy.wait()
+    other = (me // half + 1) % 2
+    for pair in range(ROWS // 2):
+        following = range(2 * pair + 2, 2 * pair + 4) if pair + 1 < ROWS // 2 else ()
+        for place in following:
+            row_copy(place).wait()
+        product = project_half(pair, other)
+        for place in following:
+            split_row(place, halves[place % 2])
+        turn_half(product, pair, other)
+        for place in following:
+            if place + ROWS < band:
+                row_copy(place + ROWS).start()
+    pl.semaphore_wait(barrier, count - 1)
+    send_group(0, 0, 0, half)
+
+    @pl.loop(0, ROWS // 2)
+    def _(pair):
+        turn_half(project_half(pair, 1 - other), pair, 1 - other)
+
+    send_group(0, 0, half, count)
+
     def transform(step):
         slot, group = step // groups, step % groups
 
@@ -595,11 +643,9 @@
             for copy in table_copies(slot):
                 copy.wait()
 
-        @pl.when(step > 0)
-        def _():
-            @pl.loop(0, ROWS // 2)
-            def _(pair):
-                turn(project(slot, group * (ROWS // 2) + pair), pair)
+        @pl.loop(0, ROWS // 2)
+        def _(pair):
+            turn(project(slot, group * (ROWS // 2) + pair), pair)
 
         @pl.when(slot == CHUNKS - 1)
         def _():
@@ -610,21 +656,7 @@
 
         @pl.when(jnp.logical_not(folded))
         def _():
-            @pl.loop(0, count)
-            def _(ahead):
-                device = (me + 1 + ahead) % count
-                rows = pl.ds(pl.multiple_of(device * ROWS * ROWS, ROWS * ROWS), ROWS * ROWS)
-                outgoing[step, rows, :] = jnp.concatenate(
-                    [turned[0, rows, :], turned[1, rows, :]], axis=1
-                ).astype(jnp.bfloat16)
-
-                @pl.when((device != me) & has_chunk(slot, device))
-                def _():
-                    order_copy(slot, group, device).start()
-
-                @pl.when((device == me) & has_chunk(slot, device))
-                def _():
-                    own_copy(slot, group).start()
+            send_group(slot, group, 0, count)
 
         @pl.when(folded)
         def _():
@@ -638,7 +670,7 @@
             def _():
                 send_pairs()
 
-    @pl.loop(0, groups + 2)
+    @pl.loop(1, groups + 2)
     def _(turn_at):
         tail = groups + (groups - 1) * (groups + 1 - turn_at)
         transform(jnp.where(turn_at < groups, turn_at, tail))
@@ -877,7 +909,11 @@
             analyse(slot)
             send_degrees(slot, crosses)
 
-        @pl.when((slot < CHUNKS - 1) | has_last)
+        @pl.when(slot == 1)
+        def _():
+            send_degrees(0, lambda device: jnp.logical_not(crosses(device)))
+
+        @pl.when(((slot < CHUNKS - 1) | has_last) & (slot > 0))
         def _():
             send_degrees(slot, lambda device: jnp.logical_not(crosses(device)))
 

time: 157 us -> 155 us (0.987)
    pallas_call x1, Pallas kernels: 149 us -> 148 us  [coefficients_of(): pl.pallas_call(functools.partial(spectral_kernel, (count, band, longitude...]
where the time goes in v5:
time: 155 us; the launch traced here: 154 us
  Pallas kernels  154 us (99%)
    pallas_call x1, Pallas kernels, coefficients_of(): pl.pallas_call(functools.partial(spectral_kernel, (count, band, longitude...  148 us
    pallas_call x1, Pallas kernels, apply_filter(): pl.pallas_call(filter_kernel, out_shape=jax.ShapeDtypeStruct((degrees, or...  5.92 us

profile of v5, /device:TPU:29, one launch (start us, length us, event | category | flops | bytes accessed | tf_op | source)
XLA Modules:
  0.0 153.7 jit_solution(5023999905647062695)
XLA Ops:
  0.0 147.8 %shard_map.100.coef_ref = bf16[44,176,256]{2,1,0:T(8,128)(2,1)} custom-call(f32[23,1440,128]{2,1,0:T(8,128)} %field_ref.1, f32[1,64]{1,0:T(1,128)} %bitcast.1, bf16[3,256,1440]{2,1,0:T(8,128)(2,1)} %constant.14.clone.high_ref, bf16[3,256,1440]{2,1,0:T(8,128)(2,1)} %constant.15.clone.low_ref, f32[384]{0:T(512)} %constant.16.clone.sine_ref, ...), custom_call_target="tpu_custom_call" | custom-call | flops 20000000000 | bytes 40000000 | tf_op jit(solution)/shard_map/pallas_call | solution.py:1037
  147.8 5.9 %shard_map.101 = bf16[22,352,256]{2,1,0:T(8,128)(2,1)} custom-call(bf16[44,176,256]{2,1,0:T(8,128)(2,1)} %shard_map.100.coef_ref, bf16[22,2,64,64]{3,2,1,0:T(8,128)(2,1)} %weight_ref.2), custom_call_target="tpu_custom_call" | custom-call | tf_op jit(solution)/shard_map/pallas_call | solution.py:1133

commit v6 on v5

--- a/solution.py
+++ b/solution.py
@@ -685,6 +685,10 @@
         def _():
             pltpu.make_async_copy(blank, out_ref.at[chunk], recv_two.at[chunk]).start()
 
+    @pl.loop(0, DEG_DEV // ROWS + 1)
+    def _(ahead):
+        chunk = me * DEG_DEV // ROWS + 1 + ahead
+        low_line = chunk * ROWS - me * DEG_DEV
         for lines_off in range(2, DEG_DEV, 2):
 
             @pl.when(low_line == lines_off)
@@ -897,10 +901,7 @@
     scales[:1] = jnp.concatenate([factor, factor], axis=1)
     scales[1:2] = jnp.concatenate([longitudes * first, jnp.zeros_like(first)], axis=1)
 
-    @pl.loop(0, 2 * groups - 2)
-    def _(turn_at):
-        late = turn_at < groups - 2
-        transform(jnp.where(late, turn_at + groups + 1, turn_at + groups + 2))
+    pl.loop(groups + 1, 2 * groups - 1)(transform)
 
     @pl.loop(0, CHUNKS)
     def _(slot):
@@ -908,6 +909,10 @@
         def _():
             analyse(slot)
             send_degrees(slot, crosses)
+
+        @pl.when(slot == 0)
+        def _():
+            pl.loop(2 * groups, CHUNKS * groups)(transform)
 
         @pl.when(slot == 1)
         def _():
@@ -964,6 +969,10 @@
         def _():
             pltpu.make_async_copy(blank, out_ref.at[chunk], recv_two.at[chunk]).wait()
 
+    @pl.loop(0, DEG_DEV // ROWS + 1)
+    def _(ahead):
+        chunk = me * DEG_DEV // ROWS + 1 + ahead
+        low_line = chunk * ROWS - me * DEG_DEV
         for lines_off in range(2, DEG_DEV, 2):
 
             @pl.when(low_line == lines_off)

time: 155 us -> 155 us (level)
  no operation moved by 1% of the time
where the time goes in v6:
time: 155 us; the launch traced here: 153 us
  Pallas kernels  153 us (99%)
    pallas_call x1, Pallas kernels, coefficients_of(): pl.pallas_call(functools.partial(spectral_kernel, (count, band, longitude...  147 us
    pallas_call x1, Pallas kernels, apply_filter(): pl.pallas_call(filter_kernel, out_shape=jax.ShapeDtypeStruct((degrees, or...  5.92 us

profile of v6, /device:TPU:29, one launch (start us, length us, event | category | flops | bytes accessed | tf_op | source)
XLA Modules:
  0.0 153.3 jit_solution(7067829645454058546)
XLA Ops:
  0.0 147.4 %shard_map.100.coef_ref = bf16[44,176,256]{2,1,0:T(8,128)(2,1)} custom-call(f32[23,1440,128]{2,1,0:T(8,128)} %field_ref.1, f32[1,64]{1,0:T(1,128)} %bitcast.1, bf16[3,256,1440]{2,1,0:T(8,128)(2,1)} %constant.14.clone.high_ref, bf16[3,256,1440]{2,1,0:T(8,128)(2,1)} %constant.15.clone.low_ref, f32[384]{0:T(512)} %constant.16.clone.sine_ref, ...), custom_call_target="tpu_custom_call" | custom-call | flops 20000000000 | bytes 40000000 | tf_op jit(solution)/shard_map/pallas_call | solution.py:1046
  147.4 5.9 %shard_map.101 = bf16[22,352,256]{2,1,0:T(8,128)(2,1)} custom-call(bf16[44,176,256]{2,1,0:T(8,128)(2,1)} %shard_map.100.coef_ref, bf16[22,2,64,64]{3,2,1,0:T(8,128)(2,1)} %weight_ref.2), custom_call_target="tpu_custom_call" | custom-call | tf_op jit(solution)/shard_map/pallas_call | solution.py:1142

commit v7 on v6

--- a/solution.py
+++ b/solution.py
@@ -786,11 +786,12 @@
     def each_target(slot, chosen, remote, local):
         first_line = owner_chunk(me, slot, count) * ROWS
 
-        @pl.loop(1, count)
+        @pl.loop(0, count)
         def _(ahead):
-            device = (me + ahead) % count
-
-            @pl.when((first_line <= device * DEG_DEV) & chosen(device))
+            device = ((me // half + 1 + ahead // half) % 2) * half + (me + ahead) % half
+            reached = first_line <= device * DEG_DEV
+
+            @pl.when(reached & chosen(device) & (device != me))
             def _():
                 remote(slot, device, 0)
 

time: 155 us -> 155 us (level); the launches traced: 153 us -> 152 us
    pallas_call x1, Pallas kernels: 147 us -> 146 us  [coefficients_of(): pl.pallas_call(functools.partial(spectral_kernel, (count, band, longitude...]
where the time goes in v7:
time: 155 us; the launch traced here: 152 us
  Pallas kernels  152 us (98%)
    pallas_call x1, Pallas kernels, coefficients_of(): pl.pallas_call(functools.partial(spectral_kernel, (count, band, longitude...  146 us
    pallas_call x1, Pallas kernels, apply_filter(): pl.pallas_call(filter_kernel, out_shape=jax.ShapeDtypeStruct((degrees, or...  5.92 us

profile of v7, /device:TPU:29, one launch (start us, length us, event | category | flops | bytes accessed | tf_op | source)
XLA Modules:
  0.0 151.8 jit_solution(4485540396296592172)
XLA Ops:
  0.0 145.8 %shard_map.100.coef_ref = bf16[44,176,256]{2,1,0:T(8,128)(2,1)} custom-call(f32[23,1440,128]{2,1,0:T(8,128)} %field_ref.1, f32[1,64]{1,0:T(1,128)} %bitcast.1, bf16[3,256,1440]{2,1,0:T(8,128)(2,1)} %constant.14.clone.high_ref, bf16[3,256,1440]{2,1,0:T(8,128)(2,1)} %constant.15.clone.low_ref, f32[384]{0:T(512)} %constant.16.clone.sine_ref, ...), custom_call_target="tpu_custom_call" | custom-call | flops 20000000000 | bytes 40000000 | tf_op jit(solution)/shard_map/pallas_call | solution.py:1047
  145.8 5.9 %shard_map.101 = bf16[22,352,256]{2,1,0:T(8,128)(2,1)} custom-call(bf16[44,176,256]{2,1,0:T(8,128)(2,1)} %shard_map.100.coef_ref, bf16[22,2,64,64]{3,2,1,0:T(8,128)(2,1)} %weight_ref.2), custom_call_target="tpu_custom_call" | custom-call | tf_op jit(solution)/shard_map/pallas_call | solution.py:1143
